TPU v7x, 256 devices: a whole 4x4x8 slice. The times are simulated.
256 devices in a mesh: ctx: 32 (over z, y_hi, core), head: 8 (over y_lo, x).
Axes of the slice: x: 4, y: 4 (y_hi: 2, y_lo: 2; y = y_hi * 2 + y_lo), z: 8, core: 2. Of those that a mesh axis runs over, the one named last changes fastest.
Arguments:
- latents: bfloat16 [16384, 4096], P('ctx', 'head')
- norm_gain: bfloat16 [4096], P('head'), may hold values from 0.5 to 2
- w_qkv: bfloat16 [4096, 32, 384], P('ctx', 'head')
- source_unit: int32 [512], replicated, may hold values from 0 to 511, as said below
- first_block: int32 [1], replicated, may hold values from 0 to 31
Outputs:
- attended: bfloat16 [16384, 32, 128], P('ctx', 'head')
Inputs may be any that keep to these rules, and one draw needn't show every extreme that they name: `source_unit`: A permutation of the 512 units. The 16 units of the sequence that one block of 512 rows holds come from 16 different encoder blocks, so one encoder block gives at most one unit to one sequence block.
All inputs are finite; a program needn't handle non-finite values.
Results may differ from a plain program's by a relative error of at most 0.0094.
Values may be sent and summed in bfloat16 or wider, within the bound.
A program may use at most 128 MiB of HBM per device.

v0:
```python
import math

import jax
import jax.numpy as jnp
from jax import lax
from jax.sharding import PartitionSpec as P

HEAD_DIM = 128
UNITS_DEV = 16
STEPS = 4


EPS = 1e-05
ROPE_BASE = 50000000.0


def shifted(value, axis, by):
    size = lax.axis_size(axis)
    return lax.ppermute(value, axis, [(i, (i + by) % size) for i in range(size)])


def rope_tables(positions, head_size):
    half = head_size // 2
    freq = jnp.exp(-math.log(ROPE_BASE) * jnp.arange(half, dtype=jnp.float32) * (2.0 / head_size))
    angles = positions.astype(jnp.float32)[:, None] * freq[None, :]
    return (jnp.cos(angles), jnp.sin(angles))


def rotate(values_in, cosine, sine):
    half = values_in.shape[-1] // 2
    left = values_in[..., :half]
    right = values_in[..., half:]
    cos_b = cosine[:, None, :]
    sin_b = sine[:, None, :]
    return jnp.concatenate([left * cos_b - right * sin_b, right * cos_b + left * sin_b], -1)


def per_device(latents, norm_gain, w_qkv, source_unit, first_block):
    cycle_size = lax.axis_size("ctx")
    own_index = lax.axis_index("ctx")
    tok_dev = latents.shape[0]
    unit = tok_dev // UNITS_DEV
    table = source_unit.reshape(cycle_size, UNITS_DEV)
    owner = table // UNITS_DEV
    mine = owner == own_index
    pick = jnp.sum(jnp.where(mine, table % UNITS_DEV, 0), axis=1)
    used = jnp.any(mine, axis=1)
    arrival = lax.dynamic_index_in_dim(owner, own_index, 0, keepdims=False)
    whole, gain = (
        lax.all_gather(latents, "head", axis=1, tiled=True),
        lax.all_gather(norm_gain, "head", axis=0, tiled=True),
    )
    units = whole.reshape(UNITS_DEV, unit, whole.shape[-1])
    chosen = jnp.take(units, pick, axis=0)
    received = lax.all_to_all(
        jnp.where(used[:, None, None], chosen, jnp.zeros_like(chosen)),
        "ctx",
        split_axis=0,
        concat_axis=0,
        tiled=True,
    )
    rows = jnp.take(received, arrival, axis=0).reshape(tok_dev, received.shape[-1])
    rows_f = rows.astype(jnp.float32)
    scale = lax.rsqrt(jnp.mean(rows_f * rows_f, -1, keepdims=True) + EPS)
    normed = (rows_f * scale * gain.astype(jnp.float32)).astype(jnp.bfloat16)
    qkv = jnp.einsum(
        "td,dhe->the",
        normed,
        lax.all_gather(w_qkv, "ctx", axis=0, tiled=True),
        preferred_element_type=jnp.float32,
    )
    block = (own_index - first_block[0]) % cycle_size
    positions = block * tok_dev + jnp.arange(tok_dev, dtype=jnp.int32)
    cosine, sine = rope_tables(positions, HEAD_DIM)
    query = rotate(qkv[..., :HEAD_DIM], cosine, sine).astype(jnp.bfloat16)
    own_keys = rotate(qkv[..., HEAD_DIM : 2 * HEAD_DIM], cosine, sine).astype(jnp.bfloat16)
    own_values = qkv[..., 2 * HEAD_DIM :].astype(jnp.bfloat16)
    own_pair = jnp.concatenate([own_keys, own_values], -1)
    received = [own_pair]
    current = own_pair
    for lag in range(1, STEPS):
        current = shifted(current, "ctx", 1)
        received.append(current)
    joined = jnp.concatenate(received[::-1], 0)
    keys = joined[..., :HEAD_DIM]
    values = joined[..., HEAD_DIM:]
    slot = jnp.arange(STEPS * tok_dev, dtype=jnp.int32)
    key_pos = (block - (STEPS - 1) + slot // tok_dev) * tok_dev + slot % tok_dev
    allowed = (key_pos[None, :] >= 0) & (key_pos[None, :] <= positions[:, None])
    scores = jnp.einsum(
        "qhe,khe->hqk", query, keys, preferred_element_type=jnp.float32
    ) * HEAD_DIM ** (-0.5)
    scores = jnp.where(allowed[None], scores, jnp.float32(-1e30))
    peak = jnp.max(scores, -1, keepdims=True)
    weights = jnp.where(allowed[None], jnp.exp(scores - peak), jnp.float32(0.0))
    total = jnp.sum(weights, -1)
    summed = jnp.einsum(
        "hqk,khe->qhe", weights.astype(jnp.bfloat16), values, preferred_element_type=jnp.float32
    )
    return (summed / jnp.transpose(total)[:, :, None]).astype(jnp.bfloat16)


def solution(mesh):
    placed = (P("ctx", "head"), P("head"), P("ctx", "head", None), P(), P())
    return jax.shard_map(
        per_device, mesh=mesh, in_specs=placed, out_specs=P("ctx", "head", None), check_vma=False
    )
```

profile of v0, /device:TPU:1, one launch (start us, length us, event | category | flops | bytes accessed | tf_op | source)
XLA Modules:
  0.0 440.1 jit_solution(8767747629120480853)
XLA Ops:
  6.5 0.0 all-gather.4.cloned.1.call-start
  6.5 0.7 all-gather.4.cloned.1.call-update
  7.3 0.0 all-gather.6.cloned.1.call-start
  7.3 2.0 copy.14
  9.3 0.0 all-gather.6.cloned.1.call-update
  9.3 0.8 reshape.215
  10.0 0.1 fusion.53
  10.2 0.1 fusion.34
  10.3 57.8 %all-gather.4.cloned.1.call-done = bf16[512,4096]{1,0:T(8,128)(2,1)} async-done(((bf16[512,512]{1,0:T(8,128)(2,1)}), bf16[512,4096]{1,0:T(8,128)(2,1)}) %all-gather.4.cloned.1.call-update) | async-done | bytes 4194320 | tf_op jit(solution)/shard_map/all_gather | solution.py:50
  68.1 7.2 %gather_fusion = bf16[32,32,4096]{2,1,0:T(8,128)(2,1)} fusion(bf16[16,32,4096]{2,1,0:T(8,128)(2,1)} %bitcast.28, s32[1024]{0:T(1024)S(1)} %pad_clamp_fusion.1), kind=kCustom, calls=%fused_computation | custom fusion | bytes 16777344 | tf_op jit(solution)/shard_map/jit(_take)/gather | solution.py:54
  75.3 7.6 %select_select_fusion = bf16[32,32,4096]{2,1,0:T(8,128)(2,1)} fusion(bf16[32,32,4096]{2,1,0:T(8,128)(2,1)} %gather_fusion, pred[32]{0:T(512)(128)(4,1)S(1)} %compare_and_fusion.1, pred[32]{0:T(512)(128)(4,1)S(1)} %get-tuple-element.5), kind=kLoop, calls=%fused_computation.12 | loop fusion | flops 8388608 | bytes 16777280 | tf_op jit(solution)/shard_map/jit(_where)/select_n | solution.py:56
  82.9 0.0 copy-start.2
  82.9 10.2 %all-to-all-start = ((bf16[32,32,4096]{2,1,0:T(8,128)(2,1)}), bf16[32,32,4096]{2,1,0:T(8,128)(2,1)}, u32[]{:S(2)}, u32[]{:S(2)}) async-start(bf16[32,32,4096]{2,1,0:T(8,128)(2,1)} %select_select_fusion), calls=%async_computation | async-start | bytes 16777216 | tf_op jit(solution)/shard_map/all_to_all | solution.py:55
  93.8 0.1 broadcast_in_dim.75
  93.9 0.1 broadcast_in_dim.76
  94.0 0.0 copy-done.2
  94.0 21.3 %all-gather = bf16[8,1,512]{2,1,0:T(2,128)(2,1)S(1)} all-gather(bf16[1,1,512]{2,1,0:T(2,128)(2,1)S(1)} %reshape.233), channel_id=1, replica_groups=mesh['ctx'=32,'head'=8] {'head'}, dimensions={0}, use_global_device_ids=true | all-gather | bytes 9216 | tf_op jit(solution)/shard_map/all_gather | solution.py:51
  115.4 0.5 multiply_cosine_fusion
  115.9 203.7 %all-to-all-done = bf16[32,32,4096]{2,1,0:T(8,128)(2,1)} async-done(((bf16[32,32,4096]{2,1,0:T(8,128)(2,1)}), bf16[32,32,4096]{2,1,0:T(8,128)(2,1)}, u32[]{:S(2)}, u32[]{:S(2)}) %all-to-all-start) | async-done | bytes 8388640 | tf_op jit(solution)/shard_map/all_to_all | solution.py:55
  319.6 6.2 %gather_fusion.1 = bf16[16,32,4096]{2,1,0:T(8,128)(2,1)} fusion(bf16[32,32,4096]{2,1,0:T(8,128)(2,1)} %all-to-all-done, s32[1024]{0:T(1024)S(1)} %pad_clamp_fusion), kind=kCustom, calls=%fused_computation.1 | custom fusion | bytes 8388672 | tf_op jit(solution)/shard_map/jit(_take)/gather | solution.py:62
  325.8 3.4 multiply_reduce_fusion
  329.2 0.1 rsqrt.12
  329.3 4.6 %bitcast_select_fusion = bf16[512,4096]{1,0:T(8,128)(2,1)} fusion(bf16[16,32,4096]{2,1,0:T(8,128)(2,1)} %gather_fusion.1, pred[512]{0:T(512)(128)(4,1)S(1)} %broadcast_in_dim.76), kind=kLoop, calls=%fused_computation.17 | loop fusion | flops 2097152 | bytes 8389120 | tf_op jit(solution)/shard_map/jit(_take)/select_n | solution.py:62
  333.9 0.0 all-gather.6.cloned.1.call-done
  333.9 10.8 %fusion.8 = f32[512,4,384]{0,2,1:T(8,128)S(1)} fusion(bf16[4096,4,384]{0,2,1:T(8,128)(2,1)} %all-gather.6.cloned.1.call-done, bf16[512,4096]{1,0:T(8,128)(2,1)} %bitcast_select_fusion, f32[4096]{0:T(1024)S(1)} %bitcast.29, f32[512]{0:T(512)S(1)} %rsqrt.12), kind=kOutput, calls=%fused_computation.15 | convolution fusion | flops 6450839552 | bytes 19941376 | tf_op jit(solution)/shard_map/td,dhe->the/dot_general | solution.py:66
  344.7 0.1 slice.65
  344.8 0.4 subtract_convert_fusion
  345.1 0.1 pad_maximum_fusion
  345.2 1.8 collective-permute-start
  347.0 11.7 %collective-permute-done = bf16[512,4,256]{0,2,1:T(8,128)(2,1)S(1)} collective-permute-done((bf16[512,4,256]{0,2,1:T(8,128)(2,1)S(1)}, bf16[512,4,256]{0,2,1:T(8,128)(2,1)S(1)}, u32[]{:S(2)}, u32[]{:S(2)}) %collective-permute-start) | collective-permute-done | bytes 1048608 | tf_op jit(solution)/shard_map/ppermute | solution.py:19
  358.8 0.0 copy-start.1
  358.8 1.0 copy-done.1
  359.8 4.0 collective-permute-start.1
  363.7 11.7 %collective-permute-done.1 = bf16[512,4,256]{0,2,1:T(8,128)(2,1)} collective-permute-done((bf16[512,4,256]{0,2,1:T(8,128)(2,1)S(1)}, bf16[512,4,256]{0,2,1:T(8,128)(2,1)}, u32[]{:S(2)}, u32[]{:S(2)}) %collective-permute-start.1) | collective-permute-done | bytes 1048608 | tf_op jit(solution)/shard_map/ppermute | solution.py:19
  375.5 4.1 collective-permute-start.2
  379.6 0.7 compare_and_fusion
  380.4 11.3 %collective-permute-done.2 = bf16[512,4,256]{0,2,1:T(8,128)(2,1)} collective-permute-done((bf16[512,4,256]{0,2,1:T(8,128)(2,1)}, bf16[512,4,256]{0,2,1:T(8,128)(2,1)}, u32[]{:S(2)}, u32[]{:S(2)}) %collective-permute-start.2) | collective-permute-done | bytes 1048608 | tf_op jit(solution)/shard_map/ppermute | solution.py:19
  391.6 2.1 maximum_maximum_fusion
  393.7 0.0 copy-start
  393.8 1.9 copy-done
  395.7 8.1 %fusion.12 = f32[4,512,2048]{2,1,0:T(8,128)} fusion(bf16[2048,4,256]{0,2,1:T(8,128)(2,1)S(1)} %maximum_maximum_fusion, bf16[512,4,64]{0,2,1:T(8,128)(2,1)S(1)} %get-tuple-element.9, bf16[512,4,64]{0,2,1:T(8,128)(2,1)S(1)} %get-tuple-element.8), kind=kOutput, calls=%fused_computation.21 | convolution fusion | flops 1074790400 | bytes 19398656 | tf_op jit(solution)/shard_map/qhe,khe->hqk/dot_general | solution.py:90
  403.8 21.5 %fusion.54 = (f32[4,512]{1,0:T(4,128)S(1)}, bf16[4,512,2048]{2,1,0:T(8,128)(2,1)}) fusion(f32[4,512,2048]{2,1,0:T(8,128)} %fusion.12, pred[512,2048]{1,0:T(8,128)(4,1)S(1)} %compare_and_fusion), kind=kOutput, calls=%fused_computation.83 | output fusion | flops 33556480 | bytes 26222592 | tf_op jit(solution)/shard_map/sub | solution.py:95
  425.3 6.9 %fusion.25 = bf16[512,4,128]{0,2,1:T(8,128)(2,1)S(1)} fusion(bf16[4,512,2048]{2,1,0:T(8,128)(2,1)} %get-tuple-element.15, bf16[2048,4,256]{0,2,1:T(8,128)(2,1)} %copy-done, f32[512,4]{0,1:T(4,128)S(1)} %bitcast.30), kind=kOutput, calls=%fused_computation.26 | convolution fusion | flops 1074266112 | bytes 11018240 | tf_op jit(solution)/shard_map/hqk,khe->qhe/dot_general | solution.py:97
  432.2 1.1 copy.17
  (14 shorter events, 0.1 us)
Async XLA Ops:
  6.5 61.6 %all-gather.4.cloned.1.call-start = ((), (), s32[]{:S(2)}) async-start(), calls=%async_computation.1 | async-start | bytes 4718592 | tf_op jit(solution)/shard_map/all_gather | solution.py:50
  7.3 326.6 %all-gather.6.cloned.1.call-start = ((), (), s32[]{:S(2)}) async-start(), calls=%async_computation.2 | async-start | bytes 12976128 | tf_op jit(solution)/shard_map/all_gather | solution.py:69
  82.9 11.1 %copy-start.2 = (bf16[512]{0:T(512)(128)(2,1)S(1)}, bf16[512]{0:T(512)(128)(2,1)}, u32[]{:S(2)}) copy-start(bf16[512]{0:T(512)(128)(2,1)} %param.6) | copy-start | bytes 3076
  82.9 236.7 %all-to-all-start = ((bf16[32,32,4096]{2,1,0:T(8,128)(2,1)}), bf16[32,32,4096]{2,1,0:T(8,128)(2,1)}, u32[]{:S(2)}, u32[]{:S(2)}) async-start(bf16[32,32,4096]{2,1,0:T(8,128)(2,1)} %select_select_fusion), calls=%async_computation | async-start | bytes 16777216 | tf_op jit(solution)/shard_map/all_to_all | solution.py:55
  345.2 13.6 %collective-permute-start = (bf16[512,4,256]{0,2,1:T(8,128)(2,1)S(1)}, bf16[512,4,256]{0,2,1:T(8,128)(2,1)S(1)}, u32[]{:S(2)}, u32[]{:S(2)}) collective-permute-start(bf16[512,4,256]{0,2,1:T(8,128)(2,1)S(1)} %pad_maximum_fusion), channel_id=1, source_target_pairs={{0,8},{8,16},{16,24},{24,32},{32,40},{40,48},{48,56},{56,64},{64,7... | collective-permute-start | bytes 3145736 | tf_op jit(solution)/shard_map/ppermute | solution.py:19
  358.8 1.0 copy-start.1
  359.8 15.7 %collective-permute-start.1 = (bf16[512,4,256]{0,2,1:T(8,128)(2,1)S(1)}, bf16[512,4,256]{0,2,1:T(8,128)(2,1)}, u32[]{:S(2)}, u32[]{:S(2)}) collective-permute-start(bf16[512,4,256]{0,2,1:T(8,128)(2,1)S(1)} %collective-permute-done), channel_id=1, source_target_pairs={{0,8},{8,16},{16,24},{24,32},{32,40},{40,48},{48,56},{56,64},{64,7... | collective-permute-start | bytes 3145736 | tf_op jit(solution)/shard_map/ppermute | solution.py:19
  375.5 16.1 %collective-permute-start.2 = (bf16[512,4,256]{0,2,1:T(8,128)(2,1)}, bf16[512,4,256]{0,2,1:T(8,128)(2,1)}, u32[]{:S(2)}, u32[]{:S(2)}) collective-permute-start(bf16[512,4,256]{0,2,1:T(8,128)(2,1)} %collective-permute-done.1), channel_id=1, source_target_pairs={{0,8},{8,16},{16,24},{24,32},{32,40},{40,48},{48,56},{56,64},{64,7... | collective-permute-start | bytes 3145736 | tf_op jit(solution)/shard_map/ppermute | solution.py:19
  393.7 1.9 copy-start
Sparse Core Ops, SparseCore 0:
  9.1 58.9 all-gather.3
  70.7 247.1 all-gather.5
where the time goes:
time: 448 us; the launch traced here: 440 us
  waiting for transfers between devices  297 us (66%)
  other arithmetic  41.3 us (9%)
  matrix products  25.9 us (6%)
  blocking collectives  21.3 us (5%)
  local copies, waits for them, and re-layouts  20.3 us (5%)
  starting transfers between devices  20.1 us (4%)
  between operations  14.2 us (3%)
    all_to_all x1, waiting for transfers between devices, per_device(): lax.all_to_all(jnp.where(used[:, None, None], chosen, jnp.zeros_like(chos...  204 us
    all_gather x1, waiting for transfers between devices, per_device(): lax.all_gather(latents, 'head', axis=1, tiled=True)  57.8 us
    ppermute x3, waiting for transfers between devices, shifted(): lax.ppermute(value, axis, [(i, (i + by) % size) for i in range(size)])  34.8 us
    sub x1, other arithmetic, per_device(): weights = jnp.where(allowed[None], jnp.exp(scores - peak), jnp.float32(0.0))  21.5 us
    all_gather x1, blocking collectives, per_device(): lax.all_gather(norm_gain, 'head', axis=0, tiled=True)  21.3 us
    dot_general x1, matrix products, per_device(): jnp.einsum('td,dhe->the', normed, lax.all_gather(w_qkv, 'ctx', axis=0, ti...  10.8 us
    all_to_all x1, starting transfers between devices, per_device(): lax.all_to_all(jnp.where(used[:, None, None], chosen, jnp.zeros_like(chos...  10.2 us
    ppermute x3, starting transfers between devices, shifted(): lax.ppermute(value, axis, [(i, (i + by) % size) for i in range(size)])  9.9 us
  transfers between devices with their start and end apart: 6, of which 5 were waited for; matrix products, arithmetic and copies ran while one was open for 8% of the time, Pallas kernels for 0%

commit v1 on v0

v1 whole, which is shorter than its diff:
```python
import math

import jax
import jax.numpy as jnp
from jax import lax
from jax.experimental import pallas as pl
from jax.experimental.pallas import tpu as pltpu
from jax.sharding import PartitionSpec as P

HEAD_DIM = 128
UNITS_DEV = 16
STEPS = 4
EPS = 1e-05
ROPE_BASE = 50000000.0

BLOCK = 512
UNIT = BLOCK // UNITS_DEV
SLICE = 512
PART = 256
NZ, NY, NX = 8, 4, 4
CYCLE = 32
WIDTH = 4096
MESH = pl.DeviceIdType.MESH
F32, BF16 = jnp.float32, jnp.bfloat16
DELTA = (0, -1, 1, 2)


def kernel(
    pick_ref, slot_ref, bias_ref, lat_ref, gain_ref, w_ref, cos_ref, sin_ref, out_ref,
    sbuf, rbuf_0, rbuf_1, xg, own_sum, all_sums, normed, wstage_kv, wstage_q, wkv, wq, acc_kv, acc_q, kvb, qb, att, mrow, lrow, obuf, oswap,
    a_send, a_recv, g_send, g_recv, x_send, x_recv, y_send, y_recv, z_send, z_recv, c_send, c_recv, h_send, h_recv,
    o_send, o_recv,
):
    ctx, head = lax.axis_index("ctx"), lax.axis_index("head")
    z, yh, c = ctx // 4, (ctx // 2) % 2, ctx % 2
    yl, x = head // 4, head % 4
    y = yh * 2 + yl

    def place(at_x, at_y):
        at_x, at_y = lax.rem(at_x + 4, 4), lax.rem(at_y + 4, 4)
        return at_y // 2, lax.rem(at_y, 2) * 4 + at_x

    def device(at_x, at_y, at_z, at_c):
        row, column = place(at_x, at_y)
        return (lax.rem(at_z + NZ, NZ) * 4 + row * 2 + at_c, column)

    right, left = device(x + 1, y, z, c), device(x - 1, y, z, c)
    up, down = device(x, y + 1, z, c), device(x, y - 1, z, c)
    above, below = device(x, y, z + 1, c), device(x, y, z - 1, c)
    sibling = device(x, y, z, 1 - c)
    partner = device(x, y + 2, z, c)

    def copy(src, dst, send, recv, to):
        return pltpu.make_async_remote_copy(
            src_ref=src, dst_ref=dst, send_sem=send, recv_sem=recv, device_id=to, device_id_type=MESH
        )

    barrier = pltpu.get_barrier_semaphore()

    @pl.loop(1, CYCLE)
    def _(step):
        pl.semaphore_signal(barrier, inc=1, device_id=(lax.rem(ctx + step, CYCLE), head), device_id_type=MESH)

    @pl.loop(1, 8)
    def _(step):
        pl.semaphore_signal(barrier, inc=1, device_id=(ctx, lax.rem(head + step, 8)), device_id_type=MESH)

    for to in (up, down):
        pl.semaphore_signal(barrier, inc=1, device_id=to, device_id_type=MESH)

    eye = lax.broadcasted_iota(jnp.int32, (128, 128), 0) == lax.broadcasted_iota(jnp.int32, (128, 128), 1)
    for at in range(4):
        rows = lat_ref[at * 128 : (at + 1) * 128].astype(F32)
        sums = jnp.sum(rows * rows, -1, keepdims=True)
        own_sum[:, at * 128 : (at + 1) * 128] = jnp.sum(jnp.where(eye, sums, 0.0), 0, keepdims=True)
    all_sums[head] = own_sum[...]
    for at in range(4):
        pair, side = at // 2, at % 2
        start = at * 384
        wstage_q[pair, :, side * 128 : (side + 1) * 128] = w_ref[:, start : start + 128]
        wstage_kv[pair, :, side * 128 : (side + 1) * 128] = w_ref[:, start + 128 : start + 256]
        wstage_kv[pair, :, 256 + side * 128 : 256 + (side + 1) * 128] = w_ref[:, start + 256 : start + 384]

    pl.semaphore_wait(barrier, CYCLE - 1 + 7 + 2)

    def sum_copy(step):
        return copy(
            own_sum, all_sums.at[head], g_send.at[step], g_recv.at[head], (ctx, lax.rem(head + step, 8))
        )

    def sum_arrival(step):
        origin = lax.rem(head + step, 8)
        return copy(own_sum, all_sums.at[origin], g_send.at[step], g_recv.at[origin], (ctx, origin))

    @pl.loop(1, 8)
    def _(step):
        sum_copy(step).start()

    stages, weights = (wstage_kv, wstage_q), (wkv, wq)

    def swap_copy(kind, row):
        return copy(
            stages[kind].at[1 - row], weights[kind].at[z, c, row], y_send.at[kind], y_recv.at[kind], partner
        )

    for kind in range(2):
        swap_copy(kind, yh).start()
        weights[kind][z, c, yh] = stages[kind][yh]

    rbuf = (rbuf_0, rbuf_1)

    def unit_copy(part, step):
        return copy(
            sbuf.at[part, step], rbuf[part].at[step], a_send.at[part], a_recv.at[part],
            (lax.rem(ctx + step, CYCLE), head),
        )

    @pl.loop(1, 8)
    def _(step):
        sum_arrival(step).wait_recv()

    total = jnp.sum(all_sums[...], 0)
    inverse = lax.rsqrt(total / WIDTH + EPS)
    gain = gain_ref[0:1].astype(F32)
    for at in range(4):
        across = jnp.broadcast_to(inverse[:, at * 128 : (at + 1) * 128], (128, 128))
        scale = jnp.sum(jnp.where(eye, across, 0.0), -1, keepdims=True)
        rows = slice(at * 128, (at + 1) * 128)
        value = (lat_ref[rows].astype(F32) * scale * gain).astype(BF16)
        normed[at * 4 : (at + 1) * 4] = value.reshape(4, UNIT, SLICE)

    for part in range(2):

        @pl.loop(0, CYCLE)
        def _(step, part=part):
            sbuf[part, step] = normed[pick_ref[step], :, part * PART : (part + 1) * PART]

        @pl.loop(1, CYCLE // 2)
        def _(step, part=part):
            unit_copy(part, step).start()
            unit_copy(part, CYCLE - step).start()

        unit_copy(part, CYCLE // 2).start()

    def x_region(part, half, first, second, quarter=None):
        at = place(first, second) if half == 0 else place(second, first)
        start, size = half * 256, 256
        if quarter is not None:
            start, size = start + quarter * 128, 128
        return xg.at[part, at[0], at[1], pl.ds(start, size), :]

    me_at = ((x, y), (y, x))
    ways = (((right, left), (up, down)), ((up, down), (right, left)))

    def x_copy(part, half, stage, s, way, receive=False):
        first, second = me_at[half]
        back = (-1 if way == 0 else 1) * (1 if receive else 0)
        on = -1 if way == 0 else 1
        if stage == 0:
            region, axis = x_region(part, half, first + back, second), 0
        elif stage == 1:
            region, axis = x_region(part, half, first + on + back, second, way), 0
        elif stage == 2:
            region, axis = x_region(part, half, first + DELTA[s], second + back), 1
        else:
            region, axis = x_region(part, half, first + DELTA[s], second + on + back, way), 1
        sem = (0, 2, 4, 12)[stage] + s * 2 + way
        return copy(
            region, region, x_send.at[part, half, sem], x_recv.at[part, half, sem], ways[half][axis][way]
        )

    def x_start(part, stage, s, way):
        for half in range(2):
            x_copy(part, half, stage, s, way).start()

    def x_wait(part, half, stage, s, way):
        x_copy(part, half, stage, s, way, receive=True).wait_recv()

    def arrange(part):
        rbuf[part][0] = sbuf[part, 0]
        copy(
            sbuf.at[part, pl.ds(1, CYCLE - 1)], rbuf[part].at[pl.ds(1, CYCLE - 1)], a_send.at[part], a_recv.at[part],
            sibling,
        ).wait_recv()
        for unit in range(UNITS_DEV):
            xg[part, yh, head, unit * UNIT : (unit + 1) * UNIT, :] = rbuf[part][slot_ref[unit]]

    def begin(part):
        for stage in (0, 2):
            for way in range(2):
                x_start(part, stage, 0, way)

    def first_axis(part):
        for way in range(2):
            for half in range(2):
                x_wait(part, half, 0, 0, way)
                x_copy(part, half, 1, 0, way).start()
        for s in (1, 2):
            for way in range(2):
                x_start(part, 2, s, way)

    def first_axis_end(part):
        for half in range(2):
            for way in range(2):
                x_wait(part, half, 1, 0, way)
        for way in range(2):
            x_start(part, 2, 3, way)

    def second_axis(part, s):
        for way in range(2):
            for half in range(2):
                x_wait(part, half, 2, s, way)
                x_copy(part, half, 3, s, way).start()

    def second_axis_end(part):
        for s in range(4):
            for half in range(2):
                for way in range(2):
                    x_wait(part, half, 3, s, way)

    def w_region(kind, at_z, row=None):
        at_z = lax.rem(at_z + NZ, NZ)
        return weights[kind].at[at_z, c] if row is None else weights[kind].at[at_z, c, row]

    def w_copy(kind, hop, way, receive=False):
        on = (-1 if way == 0 else 1) * (hop if receive else hop - 1)
        region = w_region(kind, z + on, None if hop < 4 else way)
        sem = (hop - 1) * 2 + way
        return copy(region, region, z_send.at[kind, sem], z_recv.at[kind, sem], (above, below)[way])

    def w_share(kind, at, receive=False):
        at_z = lax.rem(z + at, NZ)
        core = 1 - c if receive else c
        region = weights[kind].at[at_z, core]
        return copy(region, region, c_send.at[kind, at], c_recv.at[kind, at], sibling)

    def w_hop(kind, hop):
        if hop == 1:
            swap_copy(kind, 1 - yh).wait_recv()
            for way in range(2):
                w_copy(kind, 1, way).start()
            w_share(kind, 0).start()
            return
        for way in range(2):
            w_copy(kind, hop - 1, way, receive=True).wait_recv()
            if hop <= 4:
                w_copy(kind, hop, way).start()
            if hop - 1 < 4:
                w_share(kind, (NZ - (hop - 1)) if way == 0 else hop - 1).start()
        if hop == 5:
            w_share(kind, 4).start()

    arrange(0)
    begin(0)
    w_hop(0, 1)
    first_axis(0)
    first_axis_end(0)
    w_hop(0, 2)
    w_hop(1, 1)
    second_axis(0, 0)
    second_axis(0, 1)
    arrange(1)
    begin(1)
    w_hop(0, 3)
    second_axis(0, 2)
    second_axis(0, 3)
    w_hop(1, 2)
    first_axis(1)
    w_hop(0, 4)
    first_axis_end(1)
    w_hop(1, 3)
    second_axis_end(0)
    second_axis(1, 0)
    w_hop(0, 5)
    second_axis(1, 1)
    w_hop(1, 4)
    second_axis(1, 2)
    second_axis(1, 3)

    def project(kind, part, row):
        acc = (acc_kv, acc_q)[kind]

        def one(k):
            w_rows = jnp.concatenate([weights[kind][k, 0, part], weights[kind][k, 1, part]], 0)
            return jnp.dot(xg[part, row, k], w_rows, preferred_element_type=F32)

        if part == 0:
            acc[row] = one(0)
        else:
            acc[row] += one(0)

        @pl.loop(1, 8)
        def _(k):
            acc[row] += one(k)

    for at in range(8):
        w_share(0, at, receive=True).wait_recv()
    for row in range(2):
        project(0, 0, row)
    w_hop(1, 5)
    second_axis_end(1)

    def turn(value, row):
        return value * cos_ref[row] + pltpu.roll(value, HEAD_DIM // 2, 1) * sin_ref[row]

    def kv_region(at, side):
        return kvb.at[at, side]

    def halo(which, side, receive=False):
        if which == 0:
            src, dst, to = 5 + c, 1 + c, above
        elif which == 1:
            src, dst, to = 1 + c, 1 + c, sibling
            if receive:
                dst = 2 - c
        elif which == 2:
            src, dst, to = 3 + c, 3 + c, sibling
            if receive:
                dst = 4 - c
        elif which == 3:
            src, dst, to = 5, 5, sibling
        else:
            src, dst, to = 4, 0, device(x, y, z + 1, 0)
        return copy(kv_region(src, side), kv_region(dst, side), h_send.at[which, side], h_recv.at[which, side], to)

    for row in (1, 0):
        project(0, 1, row)
        for side in range(2):
            keys = acc_kv[row, :, side * 128 : (side + 1) * 128]
            vals = acc_kv[row, :, 256 + side * 128 : 256 + (side + 1) * 128]
            at = 2 * row + 3 + c
            kvb[at, side, 0] = turn(keys, row).astype(BF16)
            kvb[at, side, 1] = vals.astype(BF16)
            if row == 1:
                halo(0, side).start()

                @pl.when(c == 0)
                def _(side=side):
                    halo(3, side).start()

            else:

                @pl.when(c == 1)
                def _(side=side):
                    halo(4, side).start()

                halo(2, side).start()

    for at in range(8):
        w_share(1, at, receive=True).wait_recv()
    for row in (1, 0):
        project(1, 0, row)
        project(1, 1, row)
        for side in range(2):
            query = acc_q[row, :, side * 128 : (side + 1) * 128]
            qb[row, side] = turn(query, row).astype(BF16)

    def scores(query, at, side, size=BLOCK):
        keys = kvb[at, side, 0, :size]
        product = lax.dot_general(query, keys, (((1,), (1,)), ((), ())), preferred_element_type=F32)
        return product * (HEAD_DIM**-0.5 * math.log2(math.e))

    def attend(row, side, tile, lags, first):
        rows = pl.ds(tile * 256, 256)
        query = qb[row, side, rows]
        own = 2 * row + 3 + c
        pieces = []
        for lag in lags:
            if lag == 0:
                size = (tile + 1) * 256
                value = scores(query, own, side, size)
                seen = (
                    lax.broadcasted_iota(jnp.int32, (256, size), 0) + tile * 256
                    >= lax.broadcasted_iota(jnp.int32, (256, size), 1)
                )
                pieces.append((jnp.where(seen, value, -1e30), 0.0, own, size))
            else:
                pieces.append((scores(query, own - lag, side), bias_ref[row * STEPS + lag], own - lag, BLOCK))
        peak = None
        for value, bias, _, _ in pieces:
            top = jnp.max(value, -1, keepdims=True) + bias
            peak = top if peak is None else jnp.maximum(peak, top)
        if not first:
            before = mrow[row, side, rows, :1]
            peak = jnp.maximum(peak, before)
        total, summed = None, None
        for value, bias, at, size in pieces:
            weight = jnp.exp2(value - (peak - bias))
            part_total = jnp.sum(weight, -1, keepdims=True)
            part_sum = jnp.dot(weight.astype(BF16), kvb[at, side, 1, :size], preferred_element_type=F32)
            total = part_total if total is None else total + part_total
            summed = part_sum if summed is None else summed + part_sum
        if not first:
            keep = jnp.exp2(before - peak)
            total = total + lrow[row, side, rows, :1] * keep
            summed = summed + att[row, side, rows] * keep
        mrow[row, side, rows] = jnp.broadcast_to(peak, (256, 128))
        lrow[row, side, rows] = jnp.broadcast_to(total, (256, 128))
        att[row, side, rows] = summed

    def attend_all(row, side, lags, first=False):
        for tile in range(2):
            attend(row, side, tile, lags, first)

    for side in range(2):
        halo(2, side, receive=True).wait_recv()

        @pl.when(c == 1)
        def _(side=side):
            halo(3, side).wait_recv()

        attend_all(1, side, (0, 1, 2), True)
        attend_all(0, side, (0,), True)

    def pass_on(side):
        copy(
            kv_region(5 + c, side), kv_region(1 + c, side), h_send.at[0, side], h_recv.at[0, side], above
        ).wait_recv()
        halo(1, side).start()

    for side in range(2):
        pass_on(side)

    def finish(row, side):
        columns = slice(side * 128, (side + 1) * 128)
        obuf[row, :, columns] = (att[row, side] / lrow[row, side]).astype(BF16)

    def out_copy(row):
        return copy(obuf.at[1 - row], oswap, o_send.at[0], o_recv.at[0], partner)

    for side in range(2):
        halo(1, side, receive=True).wait_recv()
        attend_all(1, side, (3,))
        finish(1, side)

    @pl.when(yh == 0)
    def _():
        out_copy(0).start()

    for side in range(2):

        @pl.when(c == 0)
        def _(side=side):
            halo(4, side).wait_recv()

        attend_all(0, side, (1, 2, 3))
        finish(0, side)

    @pl.when(yh == 1)
    def _():
        out_copy(1).start()

    out_copy(yh).wait_recv()
    out_ref[yh] = obuf[yh]
    out_ref[1 - yh] = oswap[...]

    @pl.loop(1, 8)
    def _(step):
        sum_copy(step).wait_send()

    for part in range(2):
        copy(
            sbuf.at[part, pl.ds(1, CYCLE - 1)], rbuf[part].at[pl.ds(1, CYCLE - 1)], a_send.at[part], a_recv.at[part],
            sibling,
        ).wait_send()
        for half in range(2):
            for way in range(2):
                for stage in range(4):
                    for s in range(4 if stage >= 2 else 1):
                        x_copy(part, half, stage, s, way).wait_send()
    for kind in range(2):
        swap_copy(kind, yh).wait_send()
        for hop in range(1, 5):
            for way in range(2):
                w_copy(kind, hop, way).wait_send()
        for at in range(8):
            w_share(kind, at).wait_send()
    for side in range(2):
        for which in range(3):
            halo(which, side).wait_send()

        @pl.when(c == 0)
        def _(side=side):
            halo(3, side).wait_send()

        @pl.when(c == 1)
        def _(side=side):
            halo(4, side).wait_send()

    out_copy(yh).wait_send()


def per_device(latents, norm_gain, w_qkv, source_unit, first_block):
    own_index = lax.axis_index("ctx")
    table = source_unit.reshape(CYCLE, UNITS_DEV)
    owner = table // UNITS_DEV
    pick = jnp.sum(jnp.where(owner == own_index, table % UNITS_DEV, 0), axis=1)
    pick = jnp.take(pick, (own_index + jnp.arange(CYCLE, dtype=jnp.int32)) % CYCLE)
    slot = (own_index - lax.dynamic_index_in_dim(owner, own_index, 0, keepdims=False)) % CYCLE
    own_blocks = own_index // 4 * 4 + own_index % 2 + jnp.array([0, 2], jnp.int32)
    block = (own_blocks - first_block[0]) % CYCLE
    bias = jnp.where(block[:, None] >= jnp.arange(STEPS, dtype=jnp.int32)[None, :], 0.0, -1e30).astype(F32)
    half = HEAD_DIM // 2
    positions = block[:, None] * BLOCK + jnp.arange(BLOCK, dtype=jnp.int32)[None, :]
    freq = jnp.exp(-math.log(ROPE_BASE) * jnp.arange(half, dtype=F32) * (2.0 / HEAD_DIM))
    angles = positions.astype(F32)[..., None] * freq
    cosine, sine = jnp.cos(angles), jnp.sin(angles)
    cosine = jnp.concatenate([cosine, cosine], -1)
    sine = jnp.concatenate([-sine, sine], -1)
    smem, vmem = pl.BlockSpec(memory_space=pltpu.SMEM), pl.BlockSpec(memory_space=pltpu.VMEM)
    dma = pltpu.SemaphoreType.DMA
    out = pl.pallas_call(
        kernel,
        out_shape=jax.ShapeDtypeStruct((2, BLOCK, 256), BF16),
        in_specs=[smem] * 3 + [vmem] * 5,
        out_specs=vmem,
        scratch_shapes=[
            pltpu.VMEM((2, CYCLE, UNIT, PART), BF16),
            pltpu.VMEM((CYCLE, UNIT, PART), BF16),
            pltpu.VMEM((CYCLE, UNIT, PART), BF16),
            pltpu.VMEM((2, 2, 8, BLOCK, PART), BF16),
            pltpu.VMEM((1, BLOCK), F32),
            pltpu.VMEM((8, 1, BLOCK), F32),
            pltpu.VMEM((UNITS_DEV, UNIT, SLICE), BF16),
            pltpu.VMEM((2, 128, 512), BF16),
            pltpu.VMEM((2, 128, 256), BF16),
            pltpu.VMEM((NZ, 2, 2, 128, 512), BF16),
            pltpu.VMEM((NZ, 2, 2, 128, 256), BF16),
            pltpu.VMEM((2, BLOCK, 512), F32),
            pltpu.VMEM((2, BLOCK, 256), F32),
            pltpu.VMEM((7, 2, 2, BLOCK, HEAD_DIM), BF16),
            pltpu.VMEM((2, 2, BLOCK, HEAD_DIM), BF16),
            pltpu.VMEM((2, 2, BLOCK, HEAD_DIM), F32),
            pltpu.VMEM((2, 2, BLOCK, 128), F32),
            pltpu.VMEM((2, 2, BLOCK, 128), F32),
            pltpu.VMEM((2, BLOCK, 256), BF16),
            pltpu.VMEM((BLOCK, 256), BF16),
            dma((2,)), dma((2,)),
            dma((8,)), dma((8,)),
            dma((2, 2, 20)), dma((2, 2, 20)),
            dma((2,)), dma((2,)),
            dma((2, 8)), dma((2, 8)),
            dma((2, 8)), dma((2, 8)),
            dma((5, 2)), dma((5, 2)),
            dma((1,)), dma((1,)),
        ],
        compiler_params=pltpu.CompilerParams(
            collective_id=0, has_side_effects=True, vmem_limit_bytes=56 * 1024 * 1024
        ),
    )(
        pick.astype(jnp.int32), slot.astype(jnp.int32), bias.reshape(-1), latents,
        jnp.broadcast_to(norm_gain[None, :], (16, SLICE)), w_qkv.reshape(128, 4 * 384), cosine, sine,
    )
    return jnp.transpose(out.reshape(2, BLOCK, 2, HEAD_DIM), (1, 0, 2, 3)).reshape(BLOCK, 4, HEAD_DIM)


def solution(mesh):
    placed = (P("ctx", "head"), P("head"), P("ctx", "head", None), P(), P())
    return jax.shard_map(
        per_device, mesh=mesh, in_specs=placed, out_specs=P("ctx", "head", None), check_vma=False
    )
```

time: 448 us -> 126 us (0.28); the launches traced: 440 us -> 126 us
  waiting for transfers between devices: 297 us -> 0 us
  Pallas kernels: 0 us -> 115 us
  other arithmetic: 41.3 us -> 4.59 us
  matrix products: 25.9 us -> 0 us
  blocking collectives: 21.3 us -> 0 us
  starting transfers between devices: 20.1 us -> 0 us
  local copies, waits for them, and re-layouts: 20.3 us -> 5.82 us
  between operations: 14.2 us -> 0.7 us
    all_to_all x1 -> x0, waiting for transfers between devices: 204 us -> none  [per_device(): lax.all_to_all(jnp.where(used[:, None, None], chosen, jnp.zeros_like(chos...]
    pallas_call x0 -> x1, Pallas kernels: none -> 115 us  [per_device(): pl.pallas_call(kernel, out_shape=jax.ShapeDtypeStruct((2, BLOCK, 256), BF...]
    all_gather x2 -> x0, waiting for transfers between devices: 57.8 us -> none  [the longest x1 57.8 us: per_device(): lax.all_gather(latents, 'head', axis=1, tiled=True)]
    ppermute x3 -> x0, waiting for transfers between devices: 34.8 us -> none  [shifted(): lax.ppermute(value, axis, [(i, (i + by) % size) for i in range(size)])]
    dot_general x3 -> x0, matrix products: 25.9 us -> none  [the longest x1 10.8 us: per_device(): jnp.einsum('td,dhe->the', normed, lax.all_gather(w_qkv, 'ctx', axis=0, ti...]
    sub x1 -> x0, other arithmetic: 21.5 us -> none  [per_device(): weights = jnp.where(allowed[None], jnp.exp(scores - peak), jnp.float32(0.0))]
    all_gather x1 -> x0, blocking collectives: 21.3 us -> none  [per_device(): lax.all_gather(norm_gain, 'head', axis=0, tiled=True)]
    gather x2 -> x1, local copies, waits for them, and re-layouts: 13.3 us -> 0.7 us  [per_device(): jnp.take(pick, (own_index + jnp.arange(CYCLE, dtype=jnp.int32)) % CYCLE)]
  transfers between devices with their start and end apart: 6 -> 0, of which waited for: 5 -> 0; matrix products, arithmetic and copies ran while one was open for 8% -> 0% of each run, Pallas kernels for 0% -> 0%
where the time goes in v1:
time: 126 us
  Pallas kernels  115 us (91%)
  local copies, waits for them, and re-layouts  5.82 us (5%)
  other arithmetic  4.59 us (4%)
    pallas_call x1, Pallas kernels, per_device(): pl.pallas_call(kernel, out_shape=jax.ShapeDtypeStruct((2, BLOCK, 256), BF...  115 us

profile of v1, /device:TPU:1, one launch (start us, length us, event | category | flops | bytes accessed | tf_op | source)
XLA Modules:
  0.0 126.1 jit_solution(16255770790672081176)
XLA Ops:
  0.7 0.1 add_convert_fusion
  0.8 1.9 %fusion = (f32[2,512,64]{2,1,0:T(8,128)S(1)}, f32[2,512,64]{2,1,0:T(8,128)S(1)}, f32[2,512,64]{2,1,0:T(8,128)S(1)}) fusion(f32[64]{0:T(128)S(1)} %multiply_exponential_fusion, f32[2,512]{1,0:T(2,128)S(1)} %add_convert_fusion), kind=kLoop, calls=%fused_computation.5 | loop fusion | flops 131072 | bytes 790784 | tf_op jit(solution)/shard_map/neg | solution.py:509
  2.7 0.0 copy-start.1
  2.7 1.3 %pad_maximum_fusion = (f32[2,512,128]{2,1,0:T(8,128)}, f32[2,512,128]{2,1,0:T(8,128)}) fusion(f32[2,512,64]{2,1,0:T(8,128)S(1)} %get-tuple-element.11, f32[2,512,64]{2,1,0:T(8,128)S(1)} %get-tuple-element.10, f32[2,512,64]{2,1,0:T(8,128)S(1)} %get-tuple-element.9), kind=kLoop, calls=%fused_computation.3 | loop fusion | flops 262144 | bytes 1835008 | tf_op jit(solution)/shard_map/concatenate | solution.py:508
  4.0 0.0 copy-start
  4.0 0.1 compare_select_fusion.10
  4.1 0.6 select_n.101.bias_ref
  4.7 0.0 copy-done.1
  4.7 0.1 reshape.105
  4.8 0.1 add_select_fusion.1
  4.9 0.5 and_select_fusion.1.slot_ref
  5.4 0.7 gather_fusion
  6.1 0.5 and_select_fusion.3.pick_ref
  6.7 0.0 copy-done
  6.7 0.8 copy.9
  7.5 0.0 copy-start.2
  7.5 0.7 copy-done.2
  8.2 0.6 broadcast_in_dim.31.gain_ref
  8.8 115.0 %shard_map.64 = bf16[2,512,256]{2,1,0:T(8,128)(2,1)} custom-call(s32[32]{0:T(128)} %and_select_fusion.3.pick_ref, s32[16]{0:T(128)} %and_select_fusion.1.slot_ref, f32[8]{0:T(128)} %select_n.101.bias_ref, bf16[512,512]{1,0:T(8,128)(2,1)} %lat_ref.1, bf16[16,512]{1,0:T(8,128)(2,1)} %broadcast_in_dim.31.gain_ref, bf16[128,1536]{1,0:T(8,128)(2,1)} %bitcast.11, ...), custom_call_target="tpu_custom_call" | custom-call | tf_op jit(solution)/shard_map/pallas_call | solution.py:512
  123.8 1.2 reshape.107
  125.0 1.2 copy.8
  (4 shorter events, 0.0 us)
Async XLA Ops:
  2.7 2.0 %copy-start.1 = (s32[512]{0:T(512)S(1)}, s32[512]{0:T(512)}, u32[]{:S(2)}) copy-start(s32[512]{0:T(512)} %param.9) | copy-start | bytes 6148
  4.0 2.7 %copy-start = (bf16[128,4,384]{2,1,0:T(4,128)(2,1)S(1)}, bf16[128,4,384]{2,1,0:T(4,128)(2,1)}, u32[]{:S(2)}) copy-start(bf16[128,4,384]{2,1,0:T(4,128)(2,1)} %param.8) | copy-start | bytes 1179652
  7.5 0.7 copy-start.2

commit v2 on v0

v2 whole, which is shorter than its diff:
```python
import math

import jax
import jax.numpy as jnp
from jax import lax
from jax.experimental import pallas as pl
from jax.experimental.pallas import tpu as pltpu
from jax.sharding import PartitionSpec as P

HEAD_DIM = 128
UNITS_DEV = 16
STEPS = 4
EPS = 1e-05
ROPE_BASE = 50000000.0

BLOCK = 512
UNIT = BLOCK // UNITS_DEV
SLICE = 512
HALF = UNIT // 2
ROWS = BLOCK // 2
NZ, NY, NX = 8, 4, 4
CYCLE = 32
WIDTH = 4096
MESH = pl.DeviceIdType.MESH
F32, BF16 = jnp.float32, jnp.bfloat16
DELTA = (0, -1, 1, 2)
CHUNKS = ((0, 0, 512), (1, 0, 512))
SHARES = ((0, 96), (96, 160))
BASE2 = math.log2(math.e) * HEAD_DIM**-0.5


def kernel(*refs):
    unit_ref, first_ref, lat_ref, gain_ref, w_ref, far_ref, near_ref, out_ref = refs[:8]
    refs = refs[8:]
    n = len(CHUNKS)
    sbuf, rbuf, refs = refs[:n], refs[n : 2 * n], refs[2 * n :]
    (pick, ssrc, ssend, srecv, xg, own_sum, all_sums, wstage_kv, wstage_q, wkv, wq, acc_kv, acc_q, kvb, qb,
     unseen, cosine, sine, att, mrow, lrow, obuf, oswap,
     a_send, a_recv, s_send, s_recv, g_send, g_recv, x_send, x_recv, y_send, y_recv, z_send, z_recv,
     c_send, c_recv, h_send, h_recv, o_send, o_recv) = refs
    ctx, head = lax.axis_index("ctx"), lax.axis_index("head")
    z, yh, c = ctx // 4, (ctx // 2) % 2, ctx % 2
    yl, x = head // 4, head % 4
    y = yh * 2 + yl

    def place(at_x, at_y):
        at_x, at_y = lax.rem(at_x + 4, 4), lax.rem(at_y + 4, 4)
        return at_y // 2, lax.rem(at_y, 2) * 4 + at_x

    def device(at_x, at_y, at_z, at_c):
        row, column = place(at_x, at_y)
        return (lax.rem(at_z + NZ, NZ) * 4 + row * 2 + at_c, column)

    right, left = device(x + 1, y, z, c), device(x - 1, y, z, c)
    up, down = device(x, y + 1, z, c), device(x, y - 1, z, c)
    above, below = device(x, y, z + 1, c), device(x, y, z - 1, c)
    sibling = device(x, y, z, 1 - c)
    partner = device(x, y + 2, z, c)

    def copy(src, dst, send, recv, to):
        return pltpu.make_async_remote_copy(
            src_ref=src, dst_ref=dst, send_sem=send, recv_sem=recv, device_id=to, device_id_type=MESH
        )

    barrier = pltpu.get_barrier_semaphore()

    @pl.loop(1, CYCLE)
    def _(step):
        pl.semaphore_signal(barrier, inc=1, device_id=(lax.rem(ctx + step, CYCLE), head), device_id_type=MESH)

    @pl.loop(1, 8)
    def _(step):
        pl.semaphore_signal(barrier, inc=1, device_id=(ctx, lax.rem(head + step, 8)), device_id_type=MESH)

    for to in (up, down):
        pl.semaphore_signal(barrier, inc=1, device_id=to, device_id_type=MESH)

    @pl.loop(0, CYCLE)
    def _(step):
        start = lax.rem(ctx + step, CYCLE) * UNITS_DEV
        chosen = jnp.int32(0)
        for at in range(UNITS_DEV):
            value = unit_ref[start + at]
            chosen = chosen + jnp.where(lax.shift_right_logical(value, 4) == ctx, value & 15, 0)
        pick[step] = chosen

    def fill(chunk):
        part, low, high = CHUNKS[chunk]

        @pl.loop(0, CYCLE)
        def _(step):
            sbuf[chunk][step] = lat_ref[pick[step], part * HALF : (part + 1) * HALF, low:high]

    fill(0)

    eye = lax.broadcasted_iota(jnp.int32, (128, 128), 0) == lax.broadcasted_iota(jnp.int32, (128, 128), 1)
    for at in range(4):
        rows = lat_ref[at * 4 : (at + 1) * 4].astype(F32).reshape(128, SLICE)
        sums = jnp.sum(rows * rows, -1, keepdims=True)
        own_sum[:, at * 128 : (at + 1) * 128] = jnp.sum(jnp.where(eye, sums, 0.0), 0, keepdims=True)
    all_sums[head] = own_sum[...]

    pl.semaphore_wait(barrier, CYCLE - 1 + 7 + 2)

    def sum_copy(step):
        return copy(
            own_sum, all_sums.at[head], g_send.at[step], g_recv.at[head], (ctx, lax.rem(head + step, 8))
        )

    def sum_arrival(step):
        origin = lax.rem(head + step, 8)
        return copy(own_sum, all_sums.at[origin], g_send.at[step], g_recv.at[origin], (ctx, origin))

    @pl.loop(1, 8)
    def _(step):
        sum_copy(step).start()

    def unit_copy(chunk, step):
        return copy(
            sbuf[chunk].at[step], rbuf[chunk].at[step], a_send.at[chunk], a_recv.at[chunk],
            (lax.rem(ctx + step, CYCLE), head),
        )

    def units(chunk):
        others = pl.ds(1, CYCLE - 1)
        return copy(
            sbuf[chunk].at[others], rbuf[chunk].at[others], a_send.at[chunk], a_recv.at[chunk], sibling
        )

    def scale_copy(step):
        return copy(ssend.at[step], srecv.at[step], s_send.at[0], s_recv.at[0], (lax.rem(ctx + step, CYCLE), head))

    def scales():
        others = pl.ds(1, CYCLE - 1)
        return copy(ssend.at[others], srecv.at[others], s_send.at[0], s_recv.at[0], sibling)

    def to_all(one):
        @pl.loop(1, CYCLE // 2)
        def _(step):
            one(step).start()
            one(CYCLE - step).start()

        one(CYCLE // 2).start()

    def send_units(chunk):
        to_all(lambda step: unit_copy(chunk, step))

    send_units(0)

    for at in range(4):
        pair, side = at // 2, at % 2
        start = at * 384
        wstage_q[pair, :, side * 128 : (side + 1) * 128] = w_ref[:, start : start + 128]
        wstage_kv[pair, :, side * 128 : (side + 1) * 128] = w_ref[:, start + 128 : start + 256]
        wstage_kv[pair, :, 256 + side * 128 : 256 + (side + 1) * 128] = w_ref[:, start + 256 : start + 384]
    stages, weights = (wstage_kv, wstage_q), (wkv, wq)

    def swap_copy(kind, row):
        return copy(
            stages[kind].at[1 - row], weights[kind].at[z, c, row], y_send.at[kind], y_recv.at[kind], partner
        )

    for kind in range(2):
        swap_copy(kind, yh).start()
        weights[kind][z, c, yh] = stages[kind][yh]

    for chunk in range(1, n):
        fill(chunk)

    for part in range(2):
        row_at = lax.broadcasted_iota(jnp.int32, (ROWS, BLOCK), 0)
        key_at = lax.broadcasted_iota(jnp.int32, (ROWS, BLOCK), 1)
        row_pos = (row_at & ~15) * 2 + part * HALF + (row_at & 15)
        key_part = jnp.where(key_at >= ROWS, 1, 0)
        key_low = key_at - key_part * ROWS
        key_pos = (key_low & ~15) * 2 + key_part * HALF + (key_low & 15)
        unseen[part] = jnp.where(row_pos >= key_pos, 0.0, -1e30).astype(F32)

    for row in range(2):

        @pl.loop(0, 32)
        def _(at, row=row):
            far_cos, far_sin = far_ref[0, row, at], far_ref[1, row, at]
            near_cos, near_sin = near_ref[0], near_ref[1]
            to = lax.rem(at, 2) * 16 + at // 2
            cosine[row, to] = far_cos * near_cos - far_sin * near_sin
            sine[row, to] = far_sin * near_cos + far_cos * near_sin

    @pl.loop(1, 8)
    def _(step):
        sum_arrival(step).wait_recv()

    inverse = lax.rsqrt(jnp.sum(all_sums[...], 0) / WIDTH + EPS)
    for at in range(4):
        ssrc[at] = inverse[:, at * 128 : (at + 1) * 128]

    @pl.loop(0, CYCLE)
    def _(step):
        ssend[step] = ssrc[lax.shift_right_logical(pick[step], 2)]

    to_all(scale_copy)

    def x_region(chunk, half, first, second, quarter=None):
        part, low, high = CHUNKS[chunk]
        at = place(first, second) if half == 0 else place(second, first)
        start, size = SHARES[half]
        if quarter is not None:
            size = size // 2
            start += quarter * size
        return xg.at[part, at[0], at[1], pl.ds(start, size), pl.ds(low, high - low)]

    me_at = ((x, y), (y, x))
    ways = (((right, left), (up, down)), ((up, down), (right, left)))

    def x_copy(chunk, half, stage, s, way, receive=False):
        first, second = me_at[half]
        back = (-1 if way == 0 else 1) * (1 if receive else 0)
        on = -1 if way == 0 else 1
        if stage == 0:
            region, axis = x_region(chunk, half, first + back, second), 0
        elif stage == 1:
            region, axis = x_region(chunk, half, first + on + back, second, way), 0
        elif stage == 2:
            region, axis = x_region(chunk, half, first + DELTA[s], second + back), 1
        else:
            region, axis = x_region(chunk, half, first + DELTA[s], second + on + back, way), 1
        sem = (0, 2, 4, 12)[stage] + s * 2 + way
        return copy(
            region, region, x_send.at[chunk, half, sem], x_recv.at[chunk, half, sem], ways[half][axis][way]
        )

    def x_start(chunk, stage, s, way):
        for half in range(2):
            x_copy(chunk, half, stage, s, way).start()

    def x_wait(chunk, half, stage, s, way):
        x_copy(chunk, half, stage, s, way, receive=True).wait_recv()

    gain = gain_ref[...].astype(F32)
    lanes = lax.broadcasted_iota(jnp.int32, (HALF, 128), 1) - lax.broadcasted_iota(jnp.int32, (HALF, 128), 0)

    def arrange(chunk):
        part, low, high = CHUNKS[chunk]
        rbuf[chunk][0] = sbuf[chunk][0]
        units(chunk).wait_recv()
        for at in range(UNITS_DEV):
            source = unit_ref[ctx * UNITS_DEV + at]
            slot = (ctx - lax.shift_right_logical(source, 4)) & (CYCLE - 1)
            across = jnp.broadcast_to(srecv[slot], (HALF, 128))
            lane = (source & 3) * UNIT + part * HALF
            scale = jnp.sum(jnp.where(lanes == lane, across, 0.0), -1, keepdims=True)
            rows = rbuf[chunk][slot].astype(F32) * scale * gain[:, low:high]
            xg[part, yh, head, at * HALF : (at + 1) * HALF, low:high] = rows.astype(BF16)

    def begin(chunk):
        for stage in (0, 2):
            for way in range(2):
                x_start(chunk, stage, 0, way)

    def first_axis(chunk):
        for way in range(2):
            for half in range(2):
                x_wait(chunk, half, 0, 0, way)
                x_copy(chunk, half, 1, 0, way).start()
        for s in (1, 2):
            for way in range(2):
                x_start(chunk, 2, s, way)

    def first_axis_end(chunk):
        for half in range(2):
            for way in range(2):
                x_wait(chunk, half, 1, 0, way)
        for way in range(2):
            x_start(chunk, 2, 3, way)

    def second_axis(chunk, s):
        for way in range(2):
            for half in range(2):
                x_wait(chunk, half, 2, s, way)
                x_copy(chunk, half, 3, s, way).start()

    def second_axis_end(chunk):
        for s in range(4):
            for half in range(2):
                for way in range(2):
                    x_wait(chunk, half, 3, s, way)

    def w_copy(kind, hop, way, receive=False):
        on = (-1 if way == 0 else 1) * (hop if receive else hop - 1)
        region = weights[kind].at[lax.rem(z + on + NZ, NZ), c]
        sem = (hop - 1) * 2 + way
        return copy(region, region, z_send.at[kind, sem], z_recv.at[kind, sem], (above, below)[way])

    def w_share(kind, at, receive=False):
        region = weights[kind].at[lax.rem(z + at, NZ), 1 - c if receive else c]
        return copy(region, region, c_send.at[kind, at], c_recv.at[kind, at], sibling)

    def w_hop(kind, hop):
        if hop == 1:
            swap_copy(kind, 1 - yh).wait_recv()
            w_share(kind, 0).start()
        for way in range(2):
            last = 3 + way
            if 1 < hop <= last + 1:
                w_copy(kind, hop - 1, way, receive=True).wait_recv()
            if hop <= last:
                w_copy(kind, hop, way).start()
            if 1 < hop <= last + 1:
                w_share(kind, (NZ - (hop - 1)) if way == 0 else hop - 1).start()

    def project(kind, part):
        acc = (acc_kv, acc_q)[kind]

        def one(k):
            w_rows = jnp.concatenate([weights[kind][k, core, row] for row in range(2) for core in range(2)], 0)
            rows = xg[part, :, k].reshape(2 * ROWS, SLICE)
            return jnp.dot(rows, w_rows, preferred_element_type=F32)

        acc[...] = one(0)

        @pl.loop(1, 8)
        def _(k):
            acc[...] += one(k)

    def turn(value, part, row):
        places = slice(part * 16, (part + 1) * 16)
        cos_at, sin_at = cosine[row, places].reshape(ROWS, 128), sine[row, places].reshape(ROWS, 128)
        return value * cos_at + pltpu.roll(value, HEAD_DIM // 2, 1) * sin_at

    def halo(which, part, receive=False):
        if which == 0:
            src, dst, to = 5 + c, 1 + c, above
        elif which == 1:
            src, dst, to = 1 + c, 2 - c if receive else 1 + c, sibling
        elif which == 2:
            src, dst, to = 3 + c, 4 - c if receive else 3 + c, sibling
        elif which == 3:
            src, dst, to = 5, 5, sibling
        else:
            src, dst, to = 4, 0, device(x, y, z + 1, 0)
        return copy(
            kvb.at[src, part], kvb.at[dst, part], h_send.at[which, part], h_recv.at[which, part], to
        )

    def keys_values(part):
        project(0, part)
        for row in (1, 0):
            at = 2 * row + 3 + c
            rows = slice(row * ROWS, (row + 1) * ROWS)
            for side in range(2):
                keys = acc_kv[rows, side * 128 : (side + 1) * 128]
                vals = acc_kv[rows, 256 + side * 128 : 256 + (side + 1) * 128]
                kvb[at, part, side, 0] = turn(keys, part, row).astype(BF16)
                kvb[at, part, side, 1] = vals.astype(BF16)
            if row == 1:
                halo(0, part).start()

                @pl.when(c == 0)
                def _():
                    halo(3, part).start()

            else:

                @pl.when(c == 1)
                def _():
                    halo(4, part).start()

                halo(2, part).start()

    def queries(part):
        project(1, part)
        for row in range(2):
            rows = slice(row * ROWS, (row + 1) * ROWS)
            for side in range(2):
                query = acc_q[rows, side * 128 : (side + 1) * 128]
                qb[row, side, part] = turn(query, part, row).astype(BF16)

    def pass_on(part):
        halo(0, part, receive=True).wait_recv()
        halo(1, part).start()

    def block_of(at, side, kind):
        return kvb[at, :, side, kind].reshape(BLOCK, HEAD_DIM)

    def attend(row, side, tile, lags, first):
        query = qb[row, side, tile]
        own = 2 * row + 3 + c
        block = (z * 4 + 2 * row + c + CYCLE - first_ref[0]) & (CYCLE - 1)
        pieces = []
        for lag in lags:
            keys = block_of(own - lag, side, 0)
            value = lax.dot_general(query, keys, (((1,), (1,)), ((), ())), preferred_element_type=F32) * BASE2
            if lag == 0:
                pieces.append((value + unseen[tile], 0.0, own))
            else:
                pieces.append((value, jnp.where(block >= lag, 0.0, -1e30).astype(F32), own - lag))
        peak = None
        for value, bias, _ in pieces:
            top = jnp.max(value, -1, keepdims=True) + bias
            peak = top if peak is None else jnp.maximum(peak, top)
        if not first:
            before = mrow[row, side, tile, :, :1]
            peak = jnp.maximum(peak, before)
        total, summed = None, None
        for value, bias, at in pieces:
            weight = jnp.exp2(value - (peak - bias))
            part_total = jnp.sum(weight, -1, keepdims=True)
            part_sum = jnp.dot(weight.astype(BF16), block_of(at, side, 1), preferred_element_type=F32)
            total = part_total if total is None else total + part_total
            summed = part_sum if summed is None else summed + part_sum
        if not first:
            keep = jnp.exp2(before - peak)
            total = total + lrow[row, side, tile, :, :1] * keep
            summed = summed + att[row, side, tile] * keep
        return peak, total, summed

    def attend_some(row, side, lags, first=False):
        for tile in range(2):
            peak, total, summed = attend(row, side, tile, lags, first)
            mrow[row, side, tile] = jnp.broadcast_to(peak, (ROWS, 128))
            lrow[row, side, tile] = jnp.broadcast_to(total, (ROWS, 128))
            att[row, side, tile] = summed

    def attend_last(row, side, lags):
        for tile in range(2):
            _, total, summed = attend(row, side, tile, lags, False)
            obuf[row, side, :, tile] = (summed / total).astype(BF16).reshape(UNITS_DEV, HALF, HEAD_DIM)

    def out_copy(row, side):
        return copy(obuf.at[row, side], oswap.at[side], o_send.at[side], o_recv.at[side], partner)

    w_hop(0, 1)
    send_units(1)
    srecv[0] = ssend[0]
    scales().wait_recv()
    arrange(0)
    begin(0)
    w_hop(1, 1)
    first_axis(0)
    first_axis_end(0)
    w_hop(0, 2)
    second_axis(0, 0)
    second_axis(0, 1)
    w_hop(0, 3)
    second_axis(0, 2)
    second_axis(0, 3)
    arrange(1)
    begin(1)
    w_hop(1, 2)
    second_axis_end(0)
    w_hop(0, 4)
    first_axis(1)
    first_axis_end(1)
    w_hop(0, 5)
    second_axis(1, 0)
    w_hop(1, 3)
    for at in range(8):
        w_share(0, at, receive=True).wait_recv()
    keys_values(0)
    second_axis(1, 1)
    w_hop(1, 4)
    second_axis(1, 2)
    second_axis(1, 3)
    w_hop(1, 5)
    for at in range(8):
        w_share(1, at, receive=True).wait_recv()
    queries(0)
    pass_on(0)
    second_axis_end(1)
    keys_values(1)
    queries(1)
    for part in range(2):
        halo(2, part, receive=True).wait_recv()

        @pl.when(c == 1)
        def _(part=part):
            halo(3, part).wait_recv()

    for side in range(2):
        attend_some(1, side, (0, 1, 2), True)
        attend_some(0, side, (0,), True)
    pass_on(1)
    for part in range(2):
        halo(1, part, receive=True).wait_recv()
    for side in range(2):
        attend_last(1, side, (3,))

        @pl.when(yh == 0)
        def _(side=side):
            out_copy(1, side).start()

    for part in range(2):

        @pl.when(c == 0)
        def _(part=part):
            halo(4, part).wait_recv()

    for side in range(2):
        attend_last(0, side, (1, 2, 3))

        @pl.when(yh == 1)
        def _(side=side):
            out_copy(0, side).start()

    for side in range(2):
        out_ref[2 * yh + side] = obuf[yh, side].reshape(BLOCK, HEAD_DIM)
    for side in range(2):
        out_copy(yh, side).wait_recv()
        out_ref[2 - 2 * yh + side] = oswap[side].reshape(BLOCK, HEAD_DIM)

    @pl.loop(1, 8)
    def _(step):
        sum_copy(step).wait_send()

    scales().wait_send()
    for chunk in range(n):
        units(chunk).wait_send()
        for half in range(2):
            for way in range(2):
                for stage in range(4):
                    for s in range(4 if stage >= 2 else 1):
                        x_copy(chunk, half, stage, s, way).wait_send()
    for kind in range(2):
        swap_copy(kind, yh).wait_send()
        for way in range(2):
            for hop in range(1, 4 + way):
                w_copy(kind, hop, way).wait_send()
        for at in range(8):
            w_share(kind, at).wait_send()
    for part in range(2):
        for which in range(3):
            halo(which, part).wait_send()

        @pl.when(c == 0)
        def _(part=part):
            halo(3, part).wait_send()

        @pl.when(c == 1)
        def _(part=part):
            halo(4, part).wait_send()

    for side in range(2):
        out_copy(1 - yh, side).wait_send()


def per_device(latents, norm_gain, w_qkv, source_unit, first_block):
    own_index = lax.axis_index("ctx")
    own_blocks = own_index // 4 * 4 + own_index % 2 + jnp.array([0, 2], jnp.int32)
    block = (own_blocks - first_block[0]) % CYCLE
    half = HEAD_DIM // 2
    freq = jnp.exp(-math.log(ROPE_BASE) * jnp.arange(half, dtype=F32) * (2.0 / HEAD_DIM))
    freq = jnp.concatenate([freq, freq])
    sign = jnp.concatenate([-jnp.ones(half, F32), jnp.ones(half, F32)])
    starts = block[:, None] * BLOCK + 16 * jnp.arange(32, dtype=jnp.int32)[None, :]
    far = starts.astype(F32)[..., None] * freq
    near = jnp.arange(16, dtype=F32)[:, None] * freq
    far = jnp.stack([jnp.cos(far), jnp.sin(far) * sign]).reshape(2, 2, 32, 1, 128)
    near = jnp.stack([jnp.cos(near), jnp.sin(near) * sign])
    smem, vmem = pl.BlockSpec(memory_space=pltpu.SMEM), pl.BlockSpec(memory_space=pltpu.VMEM)
    dma = pltpu.SemaphoreType.DMA
    unit_slots = [pltpu.VMEM((CYCLE, HALF, high - low), BF16) for _, low, high in CHUNKS]
    n = len(CHUNKS)
    out = pl.pallas_call(
        kernel,
        out_shape=jax.ShapeDtypeStruct((4, BLOCK, HEAD_DIM), BF16),
        in_specs=[smem] * 2 + [vmem] * 5,
        out_specs=vmem,
        scratch_shapes=unit_slots
        + unit_slots
        + [
            pltpu.SMEM((CYCLE,), jnp.int32),
            pltpu.VMEM((4, 1, 128), F32),
            pltpu.VMEM((CYCLE, 1, 128), F32),
            pltpu.VMEM((CYCLE, 1, 128), F32),
            pltpu.VMEM((2, 2, 8, ROWS, SLICE), BF16),
            pltpu.VMEM((1, BLOCK), F32),
            pltpu.VMEM((8, 1, BLOCK), F32),
            pltpu.VMEM((2, 128, 512), BF16),
            pltpu.VMEM((2, 128, 256), BF16),
            pltpu.VMEM((NZ, 2, 2, 128, 512), BF16),
            pltpu.VMEM((NZ, 2, 2, 128, 256), BF16),
            pltpu.VMEM((2 * ROWS, 512), F32),
            pltpu.VMEM((2 * ROWS, 256), F32),
            pltpu.VMEM((7, 2, 2, 2, ROWS, HEAD_DIM), BF16),
            pltpu.VMEM((2, 2, 2, ROWS, HEAD_DIM), BF16),
            pltpu.VMEM((2, ROWS, BLOCK), F32),
            pltpu.VMEM((2, 32, 16, 128), F32),
            pltpu.VMEM((2, 32, 16, 128), F32),
            pltpu.VMEM((2, 2, 2, ROWS, HEAD_DIM), F32),
            pltpu.VMEM((2, 2, 2, ROWS, 128), F32),
            pltpu.VMEM((2, 2, 2, ROWS, 128), F32),
            pltpu.VMEM((2, 2, UNITS_DEV, 2, HALF, HEAD_DIM), BF16),
            pltpu.VMEM((2, UNITS_DEV, 2, HALF, HEAD_DIM), BF16),
            dma((n,)), dma((n,)),
            dma((1,)), dma((1,)),
            dma((8,)), dma((8,)),
            dma((n, 2, 20)), dma((n, 2, 20)),
            dma((2,)), dma((2,)),
            dma((2, 8)), dma((2, 8)),
            dma((2, 8)), dma((2, 8)),
            dma((5, 2)), dma((5, 2)),
            dma((2,)), dma((2,)),
        ],
        compiler_params=pltpu.CompilerParams(
            collective_id=0, has_side_effects=True, vmem_limit_bytes=56 * 1024 * 1024
        ),
    )(
        source_unit, first_block, latents.reshape(UNITS_DEV, UNIT, SLICE), norm_gain.reshape(1, SLICE),
        w_qkv.reshape(128, 4 * 384), far, near,
    )
    return jnp.transpose(out, (1, 0, 2))


def solution(mesh):
    placed = (P("ctx", "head"), P("head"), P("ctx", "head", None), P(), P())
    return jax.shard_map(
        per_device, mesh=mesh, in_specs=placed, out_specs=P("ctx", "head", None), check_vma=False
    )
```

time: 448 us -> 119 us (0.27); the launches traced: 440 us -> 118 us
  waiting for transfers between devices: 297 us -> 0 us
  Pallas kernels: 0 us -> 111 us
  other arithmetic: 41.3 us -> 1.65 us
  matrix products: 25.9 us -> 0 us
  blocking collectives: 21.3 us -> 0 us
  starting transfers between devices: 20.1 us -> 0 us
  local copies, waits for them, and re-layouts: 20.3 us -> 5.29 us
  between operations: 14.2 us -> 0.69 us
    all_to_all x1 -> x0, waiting for transfers between devices: 204 us -> none  [per_device(): lax.all_to_all(jnp.where(used[:, None, None], chosen, jnp.zeros_like(chos...]
    pallas_call x0 -> x1, Pallas kernels: none -> 111 us  [per_device(): pl.pallas_call(kernel, out_shape=jax.ShapeDtypeStruct((4, BLOCK, HEAD_DIM...]
    all_gather x2 -> x0, waiting for transfers between devices: 57.8 us -> none  [the longest x1 57.8 us: per_device(): lax.all_gather(latents, 'head', axis=1, tiled=True)]
    ppermute x3 -> x0, waiting for transfers between devices: 34.8 us -> none  [shifted(): lax.ppermute(value, axis, [(i, (i + by) % size) for i in range(size)])]
    dot_general x3 -> x0, matrix products: 25.9 us -> none  [the longest x1 10.8 us: per_device(): jnp.einsum('td,dhe->the', normed, lax.all_gather(w_qkv, 'ctx', axis=0, ti...]
    sub x1 -> x0, other arithmetic: 21.5 us -> none  [per_device(): weights = jnp.where(allowed[None], jnp.exp(scores - peak), jnp.float32(0.0))]
    all_gather x1 -> x0, blocking collectives: 21.3 us -> none  [per_device(): lax.all_gather(norm_gain, 'head', axis=0, tiled=True)]
    gather x2 -> x0, local copies, waits for them, and re-layouts: 13.3 us -> none  [the longest x1 7.18 us: per_device(): chosen = jnp.take(units, pick, axis=0)]
  transfers between devices with their start and end apart: 6 -> 0, of which waited for: 5 -> 0; matrix products, arithmetic and copies ran while one was open for 8% -> 0% of each run, Pallas kernels for 0% -> 0%
where the time goes in v2:
time: 119 us; the launch traced here: 118 us
  Pallas kernels  111 us (93%)
  local copies, waits for them, and re-layouts  5.29 us (4%)
  other arithmetic  1.65 us (1%)
    pallas_call x1, Pallas kernels, per_device(): pl.pallas_call(kernel, out_shape=jax.ShapeDtypeStruct((4, BLOCK, HEAD_DIM...  111 us
    unnamed x5, local copies, waits for them, and re-layouts  2.47 us

profile of v2, /device:TPU:1, one launch (start us, length us, event | category | flops | bytes accessed | tf_op | source)
XLA Modules:
  0.0 118.4 jit_solution(15046825354228730243)
XLA Ops:
  0.7 0.1 add_convert_fusion
  0.8 0.0 copy-start.1
  0.8 0.1 pad_maximum_fusion.2
  0.8 0.6 copy-done.1
  1.5 0.0 copy-start
  1.5 0.6 reshape.145.refs_3_
  2.0 0.1 copy-done
  2.1 0.1 fusion.1
  2.2 0.6 pad_maximum_fusion.1.refs_6_
  2.8 0.2 multiply_cosine_fusion
  3.0 0.6 pad_maximum_fusion
  3.6 1.8 %copy.8 = bf16[16,8,4,384]{3,1,2,0:T(8,128)(2,1)} copy(bf16[16,8,4,384]{3,2,1,0:T(4,128)(2,1)} %bitcast.10) | data formatting | bytes 786432
  5.4 110.7 %shard_map.64 = bf16[4,512,128]{2,1,0:T(8,128)(2,1)} custom-call(s32[512]{0:T(512)} %refs_0_.1, s32[1]{0:T(128)} %copy.9.refs_1_, bf16[16,32,512]{2,1,0:T(8,128)(2,1)} %bitcast.9, bf16[1,512]{1,0:T(2,128)(2,1)} %reshape.145.refs_3_, bf16[128,1536]{1,0:T(8,128)(2,1)} %bitcast.8, f32[2,2,32,1,128]{4,3,2,1,0:T(1,128)} %bitcast.11, ...), custom_call_target="tpu_custom_call" | custom-call | tf_op jit(solution)/shard_map/pallas_call | solution.py:563
  116.1 2.2 %copy.7 = bf16[512,4,128]{2,1,0:T(4,128)(2,1)} copy(bf16[512,4,128]{2,0,1:T(8,128)(2,1)} %bitcast.7) | data formatting | bytes 1048576 | tf_op jit(solution)/shard_map/transpose | solution.py:611
  (3 shorter events, 0.0 us)
Async XLA Ops:
  0.8 0.7 copy-start.1
  1.5 0.7 copy-start

commit v3 on v2

--- a/solution.py
+++ b/solution.py
@@ -2,6 +2,7 @@
 
 import jax
 import jax.numpy as jnp
+import numpy as np
 from jax import lax
 from jax.experimental import pallas as pl
 from jax.experimental.pallas import tpu as pltpu
@@ -24,19 +25,19 @@
 MESH = pl.DeviceIdType.MESH
 F32, BF16 = jnp.float32, jnp.bfloat16
 DELTA = (0, -1, 1, 2)
-CHUNKS = ((0, 0, 512), (1, 0, 512))
-SHARES = ((0, 96), (96, 160))
+CHUNKS = ((0, 0, 256), (0, 256, 512), (1, 0, 512))
+SHARES = ((0, 128), (128, 128))
 BASE2 = math.log2(math.e) * HEAD_DIM**-0.5
 
 
 def kernel(*refs):
-    unit_ref, first_ref, lat_ref, gain_ref, w_ref, far_ref, near_ref, out_ref = refs[:8]
+    unit_ref, first_ref, lat_ref, gain_ref, w_ref, base_ref, near_ref, out_ref = refs[:8]
     refs = refs[8:]
     n = len(CHUNKS)
     sbuf, rbuf, refs = refs[:n], refs[n : 2 * n], refs[2 * n :]
     (pick, ssrc, ssend, srecv, xg, own_sum, all_sums, wstage_kv, wstage_q, wkv, wq, acc_kv, acc_q, kvb, qb,
      unseen, cosine, sine, att, mrow, lrow, obuf, oswap,
-     a_send, a_recv, s_send, s_recv, g_send, g_recv, x_send, x_recv, y_send, y_recv, z_send, z_recv,
+     a_send, a_recv, s_send, s_recv, g_send, g_recv, x_send, x_recv, q_recv, y_send, y_recv, z_send, z_recv,
      c_send, c_recv, h_send, h_recv, o_send, o_recv) = refs
     ctx, head = lax.axis_index("ctx"), lax.axis_index("head")
     z, yh, c = ctx // 4, (ctx // 2) % 2, ctx % 2
@@ -44,12 +45,11 @@
     y = yh * 2 + yl
 
     def place(at_x, at_y):
-        at_x, at_y = lax.rem(at_x + 4, 4), lax.rem(at_y + 4, 4)
-        return at_y // 2, lax.rem(at_y, 2) * 4 + at_x
+        return lax.rem(at_y + 4, 4) * 4 + lax.rem(at_x + 4, 4)
 
     def device(at_x, at_y, at_z, at_c):
-        row, column = place(at_x, at_y)
-        return (lax.rem(at_z + NZ, NZ) * 4 + row * 2 + at_c, column)
+        at = place(at_x, at_y)
+        return (lax.rem(at_z + NZ, NZ) * 4 + at // 8 * 2 + at_c, lax.rem(at, 8))
 
     right, left = device(x + 1, y, z, c), device(x - 1, y, z, c)
     up, down = device(x, y + 1, z, c), device(x, y - 1, z, c)
@@ -104,12 +104,12 @@
 
     def sum_copy(step):
         return copy(
-            own_sum, all_sums.at[head], g_send.at[step], g_recv.at[head], (ctx, lax.rem(head + step, 8))
+            own_sum, all_sums.at[head], g_send.at[0], g_recv.at[0], (ctx, lax.rem(head + step, 8))
         )
 
-    def sum_arrival(step):
-        origin = lax.rem(head + step, 8)
-        return copy(own_sum, all_sums.at[origin], g_send.at[step], g_recv.at[origin], (ctx, origin))
+    def sums_of_others():
+        others = all_sums.at[pl.ds(0, 7)]
+        return copy(others, others, g_send.at[0], g_recv.at[0], sibling)
 
     @pl.loop(1, 8)
     def _(step):
@@ -149,10 +149,9 @@
 
     for at in range(4):
         pair, side = at // 2, at % 2
-        start = at * 384
-        wstage_q[pair, :, side * 128 : (side + 1) * 128] = w_ref[:, start : start + 128]
-        wstage_kv[pair, :, side * 128 : (side + 1) * 128] = w_ref[:, start + 128 : start + 256]
-        wstage_kv[pair, :, 256 + side * 128 : 256 + (side + 1) * 128] = w_ref[:, start + 256 : start + 384]
+        wstage_q[pair, :, side * 128 : (side + 1) * 128] = w_ref[:, at, :128]
+        wstage_kv[pair, :, side * 128 : (side + 1) * 128] = w_ref[:, at, 128:256]
+        wstage_kv[pair, :, 256 + side * 128 : 256 + (side + 1) * 128] = w_ref[:, at, 256:]
     stages, weights = (wstage_kv, wstage_q), (wkv, wq)
 
     def swap_copy(kind, row):
@@ -177,18 +176,20 @@
         unseen[part] = jnp.where(row_pos >= key_pos, 0.0, -1e30).astype(F32)
 
     for row in range(2):
+        block = (z * 4 + 2 * row + c + CYCLE - first_ref[0]) & (CYCLE - 1)
+        base_cos, base_sin = base_ref[0, block], base_ref[1, block]
 
         @pl.loop(0, 32)
-        def _(at, row=row):
-            far_cos, far_sin = far_ref[0, row, at], far_ref[1, row, at]
+        def _(at, row=row, base_cos=base_cos, base_sin=base_sin):
+            step_cos, step_sin = base_ref[0, CYCLE + at], base_ref[1, CYCLE + at]
+            far_cos = base_cos * step_cos - base_sin * step_sin
+            far_sin = base_sin * step_cos + base_cos * step_sin
             near_cos, near_sin = near_ref[0], near_ref[1]
             to = lax.rem(at, 2) * 16 + at // 2
             cosine[row, to] = far_cos * near_cos - far_sin * near_sin
             sine[row, to] = far_sin * near_cos + far_cos * near_sin
 
-    @pl.loop(1, 8)
-    def _(step):
-        sum_arrival(step).wait_recv()
+    sums_of_others().wait_recv()
 
     inverse = lax.rsqrt(jnp.sum(all_sums[...], 0) / WIDTH + EPS)
     for at in range(4):
@@ -207,7 +208,7 @@
         if quarter is not None:
             size = size // 2
             start += quarter * size
-        return xg.at[part, at[0], at[1], pl.ds(start, size), pl.ds(low, high - low)]
+        return xg.at[part, at, pl.ds(start, size), pl.ds(low, high - low)]
 
     me_at = ((x, y), (y, x))
     ways = (((right, left), (up, down)), ((up, down), (right, left)))
@@ -224,10 +225,13 @@
             region, axis = x_region(chunk, half, first + DELTA[s], second + back), 1
         else:
             region, axis = x_region(chunk, half, first + DELTA[s], second + on + back, way), 1
-        sem = (0, 2, 4, 12)[stage] + s * 2 + way
-        return copy(
-            region, region, x_send.at[chunk, half, sem], x_recv.at[chunk, half, sem], ways[half][axis][way]
-        )
+        arrived = q_recv.at[chunk] if stage == 3 else x_recv.at[chunk, half, (0, 2, 4)[stage] + s * 2 + way]
+        return copy(region, region, x_send.at[chunk], arrived, ways[half][axis][way])
+
+    def x_several(chunk, pieces):
+        part, low, high = CHUNKS[chunk]
+        region = xg.at[part, pl.ds(0, pieces), :, pl.ds(low, high - low)]
+        return copy(region, region, x_send.at[chunk], q_recv.at[chunk], right)
 
     def x_start(chunk, stage, s, way):
         for half in range(2):
@@ -236,7 +240,7 @@
     def x_wait(chunk, half, stage, s, way):
         x_copy(chunk, half, stage, s, way, receive=True).wait_recv()
 
-    gain = gain_ref[...].astype(F32)
+    gain = gain_ref[...].astype(F32).reshape(1, SLICE)
     lanes = lax.broadcasted_iota(jnp.int32, (HALF, 128), 1) - lax.broadcasted_iota(jnp.int32, (HALF, 128), 0)
 
     def arrange(chunk):
@@ -250,7 +254,7 @@
             lane = (source & 3) * UNIT + part * HALF
             scale = jnp.sum(jnp.where(lanes == lane, across, 0.0), -1, keepdims=True)
             rows = rbuf[chunk][slot].astype(F32) * scale * gain[:, low:high]
-            xg[part, yh, head, at * HALF : (at + 1) * HALF, low:high] = rows.astype(BF16)
+            xg[part, yh * 8 + head, at * HALF : (at + 1) * HALF, low:high] = rows.astype(BF16)
 
     def begin(chunk):
         for stage in (0, 2):
@@ -280,20 +284,21 @@
                 x_copy(chunk, half, 3, s, way).start()
 
     def second_axis_end(chunk):
-        for s in range(4):
-            for half in range(2):
-                for way in range(2):
-                    x_wait(chunk, half, 3, s, way)
+        x_several(chunk, 4).wait_recv()
 
     def w_copy(kind, hop, way, receive=False):
         on = (-1 if way == 0 else 1) * (hop if receive else hop - 1)
         region = weights[kind].at[lax.rem(z + on + NZ, NZ), c]
         sem = (hop - 1) * 2 + way
-        return copy(region, region, z_send.at[kind, sem], z_recv.at[kind, sem], (above, below)[way])
-
-    def w_share(kind, at, receive=False):
-        region = weights[kind].at[lax.rem(z + at, NZ), 1 - c if receive else c]
-        return copy(region, region, c_send.at[kind, at], c_recv.at[kind, at], sibling)
+        return copy(region, region, z_send.at[kind], z_recv.at[kind, sem], (above, below)[way])
+
+    def w_several(kind, pieces, send, recv):
+        region = weights[kind].at[pl.ds(0, pieces), 0]
+        return copy(region, region, send.at[kind], recv.at[kind], sibling)
+
+    def w_share(kind, at):
+        region = weights[kind].at[lax.rem(z + at, NZ), c]
+        return copy(region, region, c_send.at[kind], c_recv.at[kind], sibling)
 
     def w_hop(kind, hop):
         if hop == 1:
@@ -313,7 +318,7 @@
 
         def one(k):
             w_rows = jnp.concatenate([weights[kind][k, core, row] for row in range(2) for core in range(2)], 0)
-            rows = xg[part, :, k].reshape(2 * ROWS, SLICE)
+            rows = jnp.concatenate([xg[part, k], xg[part, 8 + k]], 0)
             return jnp.dot(rows, w_rows, preferred_element_type=F32)
 
         acc[...] = one(0)
@@ -429,44 +434,52 @@
     def out_copy(row, side):
         return copy(obuf.at[row, side], oswap.at[side], o_send.at[side], o_recv.at[side], partner)
 
+    srecv[0] = ssend[0]
+    send_units(1)
     w_hop(0, 1)
-    send_units(1)
-    srecv[0] = ssend[0]
     scales().wait_recv()
     arrange(0)
     begin(0)
+    send_units(2)
+    first_axis(0)
     w_hop(1, 1)
-    first_axis(0)
+    arrange(1)
+    begin(1)
     first_axis_end(0)
     w_hop(0, 2)
     second_axis(0, 0)
+    first_axis(1)
     second_axis(0, 1)
+    second_axis(0, 2)
+    first_axis_end(1)
+    second_axis(0, 3)
     w_hop(0, 3)
-    second_axis(0, 2)
-    second_axis(0, 3)
-    arrange(1)
-    begin(1)
+    second_axis(1, 0)
+    second_axis(1, 1)
+    second_axis_end(0)
     w_hop(1, 2)
-    second_axis_end(0)
-    w_hop(0, 4)
-    first_axis(1)
-    first_axis_end(1)
-    w_hop(0, 5)
-    second_axis(1, 0)
-    w_hop(1, 3)
-    for at in range(8):
-        w_share(0, at, receive=True).wait_recv()
-    keys_values(0)
-    second_axis(1, 1)
-    w_hop(1, 4)
+    arrange(2)
+    begin(2)
     second_axis(1, 2)
     second_axis(1, 3)
+    w_hop(0, 4)
+    second_axis_end(1)
+    first_axis(2)
+    first_axis_end(2)
+    w_hop(0, 5)
+    second_axis(2, 0)
+    w_hop(1, 3)
+    w_several(0, 8, c_send, c_recv).wait_recv()
+    keys_values(0)
+    second_axis(2, 1)
+    w_hop(1, 4)
+    second_axis(2, 2)
+    second_axis(2, 3)
     w_hop(1, 5)
-    for at in range(8):
-        w_share(1, at, receive=True).wait_recv()
+    w_several(1, 8, c_send, c_recv).wait_recv()
     queries(0)
     pass_on(0)
-    second_axis_end(1)
+    second_axis_end(2)
     keys_values(1)
     queries(1)
     for part in range(2):
@@ -508,25 +521,15 @@
         out_copy(yh, side).wait_recv()
         out_ref[2 - 2 * yh + side] = oswap[side].reshape(BLOCK, HEAD_DIM)
 
-    @pl.loop(1, 8)
-    def _(step):
-        sum_copy(step).wait_send()
-
+    sums_of_others().wait_send()
     scales().wait_send()
     for chunk in range(n):
         units(chunk).wait_send()
-        for half in range(2):
-            for way in range(2):
-                for stage in range(4):
-                    for s in range(4 if stage >= 2 else 1):
-                        x_copy(chunk, half, stage, s, way).wait_send()
+        x_several(chunk, 15).wait_send()
     for kind in range(2):
         swap_copy(kind, yh).wait_send()
-        for way in range(2):
-            for hop in range(1, 4 + way):
-                w_copy(kind, hop, way).wait_send()
-        for at in range(8):
-            w_share(kind, at).wait_send()
+        w_several(kind, 7, z_send, c_recv).wait_send()
+        w_several(kind, 8, c_send, c_recv).wait_send()
     for part in range(2):
         for which in range(3):
             halo(which, part).wait_send()
@@ -544,18 +547,17 @@
 
 
 def per_device(latents, norm_gain, w_qkv, source_unit, first_block):
-    own_index = lax.axis_index("ctx")
-    own_blocks = own_index // 4 * 4 + own_index % 2 + jnp.array([0, 2], jnp.int32)
-    block = (own_blocks - first_block[0]) % CYCLE
     half = HEAD_DIM // 2
-    freq = jnp.exp(-math.log(ROPE_BASE) * jnp.arange(half, dtype=F32) * (2.0 / HEAD_DIM))
-    freq = jnp.concatenate([freq, freq])
-    sign = jnp.concatenate([-jnp.ones(half, F32), jnp.ones(half, F32)])
-    starts = block[:, None] * BLOCK + 16 * jnp.arange(32, dtype=jnp.int32)[None, :]
-    far = starts.astype(F32)[..., None] * freq
-    near = jnp.arange(16, dtype=F32)[:, None] * freq
-    far = jnp.stack([jnp.cos(far), jnp.sin(far) * sign]).reshape(2, 2, 32, 1, 128)
-    near = jnp.stack([jnp.cos(near), jnp.sin(near) * sign])
+    freq = np.exp(-math.log(ROPE_BASE) * np.arange(half) * (2.0 / HEAD_DIM))
+    freq = np.concatenate([freq, freq])
+    sign = np.concatenate([-np.ones(half), np.ones(half)])
+
+    def table(positions):
+        angles = np.asarray(positions)[:, None] * freq
+        return np.stack([np.cos(angles), np.sin(angles) * sign]).astype(np.float32)
+
+    base = table(np.concatenate([np.arange(CYCLE) * BLOCK, np.arange(32) * 16]))[:, :, None]
+    near = table(np.arange(16))
     smem, vmem = pl.BlockSpec(memory_space=pltpu.SMEM), pl.BlockSpec(memory_space=pltpu.VMEM)
     dma = pltpu.SemaphoreType.DMA
     unit_slots = [pltpu.VMEM((CYCLE, HALF, high - low), BF16) for _, low, high in CHUNKS]
@@ -572,7 +574,7 @@
             pltpu.VMEM((4, 1, 128), F32),
             pltpu.VMEM((CYCLE, 1, 128), F32),
             pltpu.VMEM((CYCLE, 1, 128), F32),
-            pltpu.VMEM((2, 2, 8, ROWS, SLICE), BF16),
+            pltpu.VMEM((2, 16, ROWS, SLICE), BF16),
             pltpu.VMEM((1, BLOCK), F32),
             pltpu.VMEM((8, 1, BLOCK), F32),
             pltpu.VMEM((2, 128, 512), BF16),
@@ -593,11 +595,11 @@
             pltpu.VMEM((2, UNITS_DEV, 2, HALF, HEAD_DIM), BF16),
             dma((n,)), dma((n,)),
             dma((1,)), dma((1,)),
-            dma((8,)), dma((8,)),
-            dma((n, 2, 20)), dma((n, 2, 20)),
+            dma((1,)), dma((1,)),
+            dma((n,)), dma((n, 2, 12)), dma((n,)),
             dma((2,)), dma((2,)),
-            dma((2, 8)), dma((2, 8)),
-            dma((2, 8)), dma((2, 8)),
+            dma((2,)), dma((2, 8)),
+            dma((2,)), dma((2,)),
             dma((5, 2)), dma((5, 2)),
             dma((2,)), dma((2,)),
         ],
@@ -605,8 +607,8 @@
             collective_id=0, has_side_effects=True, vmem_limit_bytes=56 * 1024 * 1024
         ),
     )(
-        source_unit, first_block, latents.reshape(UNITS_DEV, UNIT, SLICE), norm_gain.reshape(1, SLICE),
-        w_qkv.reshape(128, 4 * 384), far, near,
+        source_unit, first_block, latents.reshape(UNITS_DEV, UNIT, SLICE), norm_gain,
+        w_qkv, base, near,
     )
     return jnp.transpose(out, (1, 0, 2))
 

time: 119 us -> 111 us (0.933)
  local copies, waits for them, and re-layouts: 5.29 us -> 2.24 us
  Pallas kernels: 111 us -> 108 us
  other arithmetic: 1.65 us -> 0 us
    unnamed x5 -> x0, local copies, waits for them, and re-layouts: 2.47 us -> none
    pallas_call x1, Pallas kernels: 111 us -> 108 us  [per_device(): pl.pallas_call(kernel, out_shape=jax.ShapeDtypeStruct((4, BLOCK, HEAD_DIM...]
    another operation x2 -> x0, other arithmetic: 1.23 us -> none  [the longest x1 0.63 us: per_device(): jnp.stack([jnp.cos(far), jnp.sin(far) * sign]).reshape(2, 2, 32, 1, 128)]
where the time goes in v3:
time: 111 us
  Pallas kernels  108 us (97%)
  local copies, waits for them, and re-layouts  2.24 us (2%)
    pallas_call x1, Pallas kernels, per_device(): pl.pallas_call(kernel, out_shape=jax.ShapeDtypeStruct((4, BLOCK, HEAD_DIM...  108 us
    transpose x1, local copies, waits for them, and re-layouts, per_device(): return jnp.transpose(out, (1, 0, 2))  2.24 us

profile of v3, /device:TPU:1, one launch (start us, length us, event | category | flops | bytes accessed | tf_op | source)
XLA Modules:
  0.0 111.2 jit_solution(9897079022438521293)
XLA Ops:
  0.7 108.3 %shard_map.73 = bf16[4,512,128]{2,1,0:T(8,128)(2,1)} custom-call(s32[512]{0:T(512)} %refs_0_.1, s32[1]{0:T(128)S(6)} %copy.9.refs_1_, bf16[16,32,512]{2,1,0:T(8,128)(2,1)} %bitcast.3, bf16[512]{0:T(512)(128)(2,1)} %refs_3_.1, bf16[128,4,384]{2,1,0:T(4,128)(2,1)} %refs_4_.1, f32[2,64,1,128]{3,2,1,0:T(1,128)} %constant.4.clone.refs_5_, ...), custom_call_target="tpu_custom_call" | custom-call | tf_op jit(solution)/shard_map/pallas_call | solution.py:565
  109.0 2.2 %copy.8 = bf16[512,4,128]{2,1,0:T(4,128)(2,1)} copy(bf16[512,4,128]{2,0,1:T(8,128)(2,1)} %bitcast.2) | data formatting | bytes 1048576 | tf_op jit(solution)/shard_map/transpose | solution.py:613

commit v4 on v3

--- a/solution.py
+++ b/solution.py
@@ -347,9 +347,25 @@
             kvb.at[src, part], kvb.at[dst, part], h_send.at[which, part], h_recv.at[which, part], to
         )
 
+    def project_keys_values(part, row):
+        acc = acc_kv.at[row * ROWS : (row + 1) * ROWS]
+
+        def one(k):
+            w_rows = jnp.concatenate([wkv[k, core, half] for half in range(2) for core in range(2)], 0)
+            return jnp.dot(xg[part, 8 * row + k], w_rows, preferred_element_type=F32)
+
+        acc[...] = one(0)
+
+        @pl.loop(1, 8)
+        def _(k):
+            acc[...] += one(k)
+
     def keys_values(part):
-        project(0, part)
+        if part == 0:
+            project(0, part)
         for row in (1, 0):
+            if part == 1:
+                project_keys_values(part, row)
             at = 2 * row + 3 + c
             rows = slice(row * ROWS, (row + 1) * ROWS)
             for side in range(2):
@@ -495,13 +511,14 @@
     pass_on(1)
     for part in range(2):
         halo(1, part, receive=True).wait_recv()
+    @pl.when(yh == 0)
+    def _():
+        for side in range(2):
+            attend_last(1, side, (3,))
+            out_copy(1, side).start()
+
     for side in range(2):
-        attend_last(1, side, (3,))
-
-        @pl.when(yh == 0)
-        def _(side=side):
-            out_copy(1, side).start()
-
+        attend_some(0, side, (1, 2))
     for part in range(2):
 
         @pl.when(c == 0)
@@ -509,11 +526,16 @@
             halo(4, part).wait_recv()
 
     for side in range(2):
-        attend_last(0, side, (1, 2, 3))
+        attend_last(0, side, (3,))
 
         @pl.when(yh == 1)
         def _(side=side):
             out_copy(0, side).start()
+
+    @pl.when(yh == 1)
+    def _():
+        for side in range(2):
+            attend_last(1, side, (3,))
 
     for side in range(2):
         out_ref[2 * yh + side] = obuf[yh, side].reshape(BLOCK, HEAD_DIM)

time: 111 us -> 110 us (level)
  no operation moved by 1% of the time
where the time goes in v4:
time: 110 us
  Pallas kernels  107 us (97%)
  local copies, waits for them, and re-layouts  2.24 us (2%)
    pallas_call x1, Pallas kernels, per_device(): pl.pallas_call(kernel, out_shape=jax.ShapeDtypeStruct((4, BLOCK, HEAD_DIM...  107 us
    transpose x1, local copies, waits for them, and re-layouts, per_device(): return jnp.transpose(out, (1, 0, 2))  2.24 us

profile of v4, /device:TPU:1, one launch (start us, length us, event | category | flops | bytes accessed | tf_op | source)
XLA Modules:
  0.0 110.1 jit_solution(1730366612654077945)
XLA Ops:
  0.7 107.2 %shard_map.73 = bf16[4,512,128]{2,1,0:T(8,128)(2,1)} custom-call(s32[512]{0:T(512)} %refs_0_.1, s32[1]{0:T(128)S(6)} %copy.9.refs_1_, bf16[16,32,512]{2,1,0:T(8,128)(2,1)} %bitcast.3, bf16[512]{0:T(512)(128)(2,1)} %refs_3_.1, bf16[128,4,384]{2,1,0:T(4,128)(2,1)} %refs_4_.1, f32[2,64,1,128]{3,2,1,0:T(1,128)} %constant.4.clone.refs_5_, ...), custom_call_target="tpu_custom_call" | custom-call | tf_op jit(solution)/shard_map/pallas_call | solution.py:587
  107.9 2.2 %copy.8 = bf16[512,4,128]{2,1,0:T(4,128)(2,1)} copy(bf16[512,4,128]{2,0,1:T(8,128)(2,1)} %bitcast.2) | data formatting | bytes 1048576 | tf_op jit(solution)/shard_map/transpose | solution.py:635

commit v5 on v4

--- a/solution.py
+++ b/solution.py
@@ -451,8 +451,8 @@
         return copy(obuf.at[row, side], oswap.at[side], o_send.at[side], o_recv.at[side], partner)
 
     srecv[0] = ssend[0]
+    w_hop(0, 1)
     send_units(1)
-    w_hop(0, 1)
     scales().wait_recv()
     arrange(0)
     begin(0)

time: 110 us -> 113 us (1.027)
  Pallas kernels: 107 us -> 109 us
    pallas_call x1, Pallas kernels: 107 us -> 109 us  [per_device(): pl.pallas_call(kernel, out_shape=jax.ShapeDtypeStruct((4, BLOCK, HEAD_DIM...]
where the time goes in v5:
time: 113 us; the launch traced here: 112 us
  Pallas kernels  109 us (96%)
  local copies, waits for them, and re-layouts  2.24 us (2%)
    pallas_call x1, Pallas kernels, per_device(): pl.pallas_call(kernel, out_shape=jax.ShapeDtypeStruct((4, BLOCK, HEAD_DIM...  109 us

profile of v5, /device:TPU:1, one launch (start us, length us, event | category | flops | bytes accessed | tf_op | source)
XLA Modules:
  0.0 112.4 jit_solution(6560762516952090026)
XLA Ops:
  0.7 109.5 %shard_map.73 = bf16[4,512,128]{2,1,0:T(8,128)(2,1)} custom-call(s32[512]{0:T(512)} %refs_0_.1, s32[1]{0:T(128)S(6)} %copy.9.refs_1_, bf16[16,32,512]{2,1,0:T(8,128)(2,1)} %bitcast.3, bf16[512]{0:T(512)(128)(2,1)} %refs_3_.1, bf16[128,4,384]{2,1,0:T(4,128)(2,1)} %refs_4_.1, f32[2,64,1,128]{3,2,1,0:T(1,128)} %constant.4.clone.refs_5_, ...), custom_call_target="tpu_custom_call" | custom-call | tf_op jit(solution)/shard_map/pallas_call | solution.py:587
  110.1 2.2 %copy.8 = bf16[512,4,128]{2,1,0:T(4,128)(2,1)} copy(bf16[512,4,128]{2,0,1:T(8,128)(2,1)} %bitcast.2) | data formatting | bytes 1048576 | tf_op jit(solution)/shard_map/transpose | solution.py:635
